TPU v7x, 128 devices: a whole 4x4x4 slice. The times are simulated.
128 devices in a mesh: section: 4 (over y), expert: 32 (over x, z, core).
Axes of the slice: x: 4, y: 4, z: 4, core: 2. Of those that a mesh axis runs over, the one named last changes fastest.
Arguments:
- tokens: bfloat16 [4, 1024, 4096], P('section', 'expert'), may hold values from -6 to 6
- w_in: bfloat16 [2, 4, 2, 4096, 12288], P(None, 'section', None, None, 'expert'), may hold values from -0.09375 to 0.09375
- w_down: bfloat16 [2, 4, 12288, 4096], P(None, 'section', 'expert'), may hold values from -0.15625 to 0.15625
- norm_gain: float32 [2, 4, 4096], P(None, 'section'), may hold values from 0.1 to 1.9
- route_ids: int32 [2, 4, 4, 1024, 8], P(None, 'section', None, 'expert'), may hold values from 0 to 127, as said below
- gate_values: float32 [2, 4, 4, 1024, 8], P(None, 'section', None, 'expert'), may hold values from 0.4 to 1.6
Outputs:
- mixed: bfloat16 [4, 1024, 4096], P('section', 'expert')
Inputs may be any that keep to these rules, and one draw needn't show every extreme that they name: `route_ids`: each row names 8 different experts; among the 32 rows of one device for one layer and micro-batch, no expert is named by more than 4 rows; in every layer and micro-batch some expert below 8 is named by exactly 4 rows of every device.
All inputs are finite; a program needn't handle non-finite values.
Results may differ from a plain program's by a relative error of at most 0.04.
Values may be sent and summed in bfloat16 or wider, within the bound.
No kernel may reach another device: no remote copies, remote signals or barrier semaphores. Data moves between devices by JAX's collectives and lax.ppermute only.
A program may use at most 64 MiB of HBM per device.

v0:
```python
import jax
import jax.numpy as jnp
from jax import lax
from jax.sharding import PartitionSpec as P

SPLIT = 4
CAP = 4


def from_behind(x, axis, by):
    count = lax.axis_size(axis)
    return lax.ppermute(x, axis, [(i, (i + by) % count) for i in range(count)])


def row_slots(route_rows, gate_rows, n_window, capacity):
    window = jnp.arange(n_window, dtype=jnp.int32)
    match_table = route_rows[:, :, None] == window[None, None, :]
    chosen = jnp.any(match_table, axis=1)
    weight = jnp.sum(jnp.where(match_table, gate_rows[:, :, None], jnp.float32(0.0)), axis=1)
    position = jnp.cumsum(chosen.astype(jnp.int32), axis=0) - 1
    places = jnp.arange(capacity, dtype=jnp.int32)
    onehot = jnp.logical_and(position[:, :, None] == places[None, None, :], chosen[:, :, None])
    return (onehot, weight)


def normalize(values, gain):
    scale = lax.rsqrt(jnp.mean(values * values, axis=-1, keepdims=True) + 1e-06)
    return (values * scale * gain).astype(jnp.bfloat16)


def body(tokens, w_in, w_down, norm_gain, route_ids, gate_values):
    sections = lax.axis_size("section")
    members = lax.axis_size("expert")
    n_window = members // SPLIT
    layers = w_in.shape[0] * sections
    section_index = lax.axis_index("section")
    width = tokens.shape[-1]
    capacity = CAP

    def run_layer(state, repeat, micro):
        routes = route_ids[repeat, 0, micro]
        gates = gate_values[repeat, 0, micro]
        onehot, weight = row_slots(routes, gates, n_window, capacity)
        values = state.astype(jnp.float32)
        gain = norm_gain[repeat, 0]
        weight_in = w_in[repeat, 0]
        weight_down = w_down[repeat, 0]
        source = normalize(values, gain)
        table = onehot.astype(jnp.bfloat16)
        packed = jnp.einsum(
            "rec,rd->ecd", table, source, preferred_element_type=jnp.float32
        ).astype(jnp.bfloat16)
        outgoing = jnp.broadcast_to(packed[:, None], (n_window, SPLIT, capacity, width)).reshape(
            members, capacity, width
        )
        incoming = lax.all_to_all(outgoing, "expert", split_axis=0, concat_axis=0, tiled=True)
        count = incoming.shape[1]
        flat = incoming.reshape(members * count, width)
        gate = jnp.dot(flat, weight_in[0], preferred_element_type=jnp.float32)
        upward = jnp.dot(flat, weight_in[1], preferred_element_type=jnp.float32)
        hidden = (jax.nn.silu(gate) * upward).astype(jnp.bfloat16)
        partial_out = jnp.dot(hidden, weight_down, preferred_element_type=jnp.float32).astype(
            jnp.bfloat16
        )
        partial_out = partial_out.reshape(members, count, width)
        returned = lax.all_to_all(partial_out, "expert", split_axis=0, concat_axis=0, tiled=True)
        outputs = jnp.sum(
            returned.reshape(n_window, SPLIT, capacity, width).astype(jnp.float32), axis=1
        )
        mixing = onehot.astype(jnp.float32) * weight[:, :, None]
        update = jnp.einsum("rec,ecd->rd", mixing, outputs)
        return (values + update).astype(jnp.bfloat16)

    def advance(moment, state):
        micro = (section_index - moment) % sections
        start = (sections - micro) % sections
        level = moment - start
        active = jnp.logical_and(level >= 0, level < layers)
        repeat = jnp.clip(level, 0, layers - 1) // sections
        updated = run_layer(state, repeat, micro)
        state = jnp.where(active, updated, state)
        return from_behind(state, "section", 1)

    state = lax.fori_loop(0, layers + sections - 1, advance, tokens[0])
    state = from_behind(state, "section", 1)
    return state[None]


def solution(mesh):
    return jax.shard_map(
        body,
        mesh=mesh,
        in_specs=(
            P("section", "expert", None),
            P(None, "section", None, None, "expert"),
            P(None, "section", "expert", None),
            P(None, "section", None),
            P(None, "section", None, "expert", None),
            P(None, "section", None, "expert", None),
        ),
        out_specs=P("section", "expert", None),
        check_vma=False,
    )
```

profile of v0, /device:TPU:8, one launch (start us, length us, event | category | flops | bytes accessed | tf_op | source)
XLA Modules:
  0.0 721.7 jit_solution(15535601166517033839)
XLA Ops:
  1.0 711.1 %while.16 = (s32[]{:T(128)}, bf16[32,4096]{1,0:T(8,128)(2,1)S(1)}, s32[]{:T(128)}, s32[2,1,4,32,8]{3,4,2,1,0:T(8,128)}, f32[2,1,4,32,8]{3,4,2,1,0:T(8,128)}, /*i...) while((s32[]{:T(128)}, bf16[32,4096]{1,0:T(8,128)(2,1)S(1)}, ...), condition=%wide.region_6.7_spmd, body=%wide.region_0.6_spmd.sunk | while | flops 1228069632 | bytes 29301480 | solution.py:84
  13.0 16.8 %all-to-all-done = bf16[32,4,4096]{2,1,0:T(4,128)(2,1)S(1)} async-done(((bf16[32,4,4096]{2,1,0:T(4,128)(2,1)}), bf16[32,4,4096]{2,1,0:T(4,128)(2,1)S(1)}, u32[]{:S(2)}, u32[]{:S(2)}) %all-to-all-start) | async-done | bytes 1048608 | tf_op jit(solution)/shard_map/while/body/eval_jaxpr/all_to_all | solution.py:56
  42.9 16.1 %all-to-all-done.1 = bf16[32,4,4096]{2,1,0:T(4,128)(2,1)S(1)} async-done(((bf16[32,4,4096]{2,1,0:T(4,128)(2,1)}), bf16[32,4,4096]{2,1,0:T(4,128)(2,1)S(1)}, u32[]{:S(2)}, u32[]{:S(2)}) %all-to-all-start.1) | async-done | bytes 1048608 | tf_op jit(solution)/shard_map/while/body/eval_jaxpr/all_to_all | solution.py:66
  76.3 16.8 %all-to-all-done = bf16[32,4,4096]{2,1,0:T(4,128)(2,1)S(1)} async-done(((bf16[32,4,4096]{2,1,0:T(4,128)(2,1)}), bf16[32,4,4096]{2,1,0:T(4,128)(2,1)S(1)}, u32[]{:S(2)}, u32[]{:S(2)}) %all-to-all-start) | async-done | bytes 1048608 | tf_op jit(solution)/shard_map/while/body/eval_jaxpr/all_to_all | solution.py:56
  106.2 16.1 %all-to-all-done.1 = bf16[32,4,4096]{2,1,0:T(4,128)(2,1)S(1)} async-done(((bf16[32,4,4096]{2,1,0:T(4,128)(2,1)}), bf16[32,4,4096]{2,1,0:T(4,128)(2,1)S(1)}, u32[]{:S(2)}, u32[]{:S(2)}) %all-to-all-start.1) | async-done | bytes 1048608 | tf_op jit(solution)/shard_map/while/body/eval_jaxpr/all_to_all | solution.py:66
  139.5 16.8 %all-to-all-done = bf16[32,4,4096]{2,1,0:T(4,128)(2,1)S(1)} async-done(((bf16[32,4,4096]{2,1,0:T(4,128)(2,1)}), bf16[32,4,4096]{2,1,0:T(4,128)(2,1)S(1)}, u32[]{:S(2)}, u32[]{:S(2)}) %all-to-all-start) | async-done | bytes 1048608 | tf_op jit(solution)/shard_map/while/body/eval_jaxpr/all_to_all | solution.py:56
  169.4 16.1 %all-to-all-done.1 = bf16[32,4,4096]{2,1,0:T(4,128)(2,1)S(1)} async-done(((bf16[32,4,4096]{2,1,0:T(4,128)(2,1)}), bf16[32,4,4096]{2,1,0:T(4,128)(2,1)S(1)}, u32[]{:S(2)}, u32[]{:S(2)}) %all-to-all-start.1) | async-done | bytes 1048608 | tf_op jit(solution)/shard_map/while/body/eval_jaxpr/all_to_all | solution.py:66
  204.0 16.8 %all-to-all-done = bf16[32,4,4096]{2,1,0:T(4,128)(2,1)S(1)} async-done(((bf16[32,4,4096]{2,1,0:T(4,128)(2,1)}), bf16[32,4,4096]{2,1,0:T(4,128)(2,1)S(1)}, u32[]{:S(2)}, u32[]{:S(2)}) %all-to-all-start) | async-done | bytes 1048608 | tf_op jit(solution)/shard_map/while/body/eval_jaxpr/all_to_all | solution.py:56
  233.9 16.1 %all-to-all-done.1 = bf16[32,4,4096]{2,1,0:T(4,128)(2,1)S(1)} async-done(((bf16[32,4,4096]{2,1,0:T(4,128)(2,1)}), bf16[32,4,4096]{2,1,0:T(4,128)(2,1)S(1)}, u32[]{:S(2)}, u32[]{:S(2)}) %all-to-all-start.1) | async-done | bytes 1048608 | tf_op jit(solution)/shard_map/while/body/eval_jaxpr/all_to_all | solution.py:66
  251.3 9.4 %collective-permute-done = bf16[32,4096]{1,0:T(8,128)(2,1)S(1)} collective-permute-done((bf16[32,4096]{1,0:T(8,128)(2,1)S(1)}, bf16[32,4096]{1,0:T(8,128)(2,1)S(1)}, u32[]{:S(2)}, u32[]{:S(2)}) %collective-permute-start) | collective-permute-done | bytes 262176 | tf_op jit(solution)/shard_map/while/body/eval_jaxpr/ppermute | solution.py:12
  268.5 16.8 %all-to-all-done = bf16[32,4,4096]{2,1,0:T(4,128)(2,1)S(1)} async-done(((bf16[32,4,4096]{2,1,0:T(4,128)(2,1)}), bf16[32,4,4096]{2,1,0:T(4,128)(2,1)S(1)}, u32[]{:S(2)}, u32[]{:S(2)}) %all-to-all-start) | async-done | bytes 1048608 | tf_op jit(solution)/shard_map/while/body/eval_jaxpr/all_to_all | solution.py:56
  298.4 16.1 %all-to-all-done.1 = bf16[32,4,4096]{2,1,0:T(4,128)(2,1)S(1)} async-done(((bf16[32,4,4096]{2,1,0:T(4,128)(2,1)}), bf16[32,4,4096]{2,1,0:T(4,128)(2,1)S(1)}, u32[]{:S(2)}, u32[]{:S(2)}) %all-to-all-start.1) | async-done | bytes 1048608 | tf_op jit(solution)/shard_map/while/body/eval_jaxpr/all_to_all | solution.py:66
  315.4 9.8 %collective-permute-done = bf16[32,4096]{1,0:T(8,128)(2,1)S(1)} collective-permute-done((bf16[32,4096]{1,0:T(8,128)(2,1)S(1)}, bf16[32,4096]{1,0:T(8,128)(2,1)S(1)}, u32[]{:S(2)}, u32[]{:S(2)}) %collective-permute-start) | collective-permute-done | bytes 262176 | tf_op jit(solution)/shard_map/while/body/eval_jaxpr/ppermute | solution.py:12
  332.9 16.8 %all-to-all-done = bf16[32,4,4096]{2,1,0:T(4,128)(2,1)S(1)} async-done(((bf16[32,4,4096]{2,1,0:T(4,128)(2,1)}), bf16[32,4,4096]{2,1,0:T(4,128)(2,1)S(1)}, u32[]{:S(2)}, u32[]{:S(2)}) %all-to-all-start) | async-done | bytes 1048608 | tf_op jit(solution)/shard_map/while/body/eval_jaxpr/all_to_all | solution.py:56
  362.8 16.1 %all-to-all-done.1 = bf16[32,4,4096]{2,1,0:T(4,128)(2,1)S(1)} async-done(((bf16[32,4,4096]{2,1,0:T(4,128)(2,1)}), bf16[32,4,4096]{2,1,0:T(4,128)(2,1)S(1)}, u32[]{:S(2)}, u32[]{:S(2)}) %all-to-all-start.1) | async-done | bytes 1048608 | tf_op jit(solution)/shard_map/while/body/eval_jaxpr/all_to_all | solution.py:66
  379.8 9.8 %collective-permute-done = bf16[32,4096]{1,0:T(8,128)(2,1)S(1)} collective-permute-done((bf16[32,4096]{1,0:T(8,128)(2,1)S(1)}, bf16[32,4096]{1,0:T(8,128)(2,1)S(1)}, u32[]{:S(2)}, u32[]{:S(2)}) %collective-permute-start) | collective-permute-done | bytes 262176 | tf_op jit(solution)/shard_map/while/body/eval_jaxpr/ppermute | solution.py:12
  397.4 16.8 %all-to-all-done = bf16[32,4,4096]{2,1,0:T(4,128)(2,1)S(1)} async-done(((bf16[32,4,4096]{2,1,0:T(4,128)(2,1)}), bf16[32,4,4096]{2,1,0:T(4,128)(2,1)S(1)}, u32[]{:S(2)}, u32[]{:S(2)}) %all-to-all-start) | async-done | bytes 1048608 | tf_op jit(solution)/shard_map/while/body/eval_jaxpr/all_to_all | solution.py:56
  427.3 16.1 %all-to-all-done.1 = bf16[32,4,4096]{2,1,0:T(4,128)(2,1)S(1)} async-done(((bf16[32,4,4096]{2,1,0:T(4,128)(2,1)}), bf16[32,4,4096]{2,1,0:T(4,128)(2,1)S(1)}, u32[]{:S(2)}, u32[]{:S(2)}) %all-to-all-start.1) | async-done | bytes 1048608 | tf_op jit(solution)/shard_map/while/body/eval_jaxpr/all_to_all | solution.py:66
  444.3 9.8 %collective-permute-done = bf16[32,4096]{1,0:T(8,128)(2,1)S(1)} collective-permute-done((bf16[32,4096]{1,0:T(8,128)(2,1)S(1)}, bf16[32,4096]{1,0:T(8,128)(2,1)S(1)}, u32[]{:S(2)}, u32[]{:S(2)}) %collective-permute-start) | collective-permute-done | bytes 262176 | tf_op jit(solution)/shard_map/while/body/eval_jaxpr/ppermute | solution.py:12
  461.9 16.8 %all-to-all-done = bf16[32,4,4096]{2,1,0:T(4,128)(2,1)S(1)} async-done(((bf16[32,4,4096]{2,1,0:T(4,128)(2,1)}), bf16[32,4,4096]{2,1,0:T(4,128)(2,1)S(1)}, u32[]{:S(2)}, u32[]{:S(2)}) %all-to-all-start) | async-done | bytes 1048608 | tf_op jit(solution)/shard_map/while/body/eval_jaxpr/all_to_all | solution.py:56
  491.8 16.1 %all-to-all-done.1 = bf16[32,4,4096]{2,1,0:T(4,128)(2,1)S(1)} async-done(((bf16[32,4,4096]{2,1,0:T(4,128)(2,1)}), bf16[32,4,4096]{2,1,0:T(4,128)(2,1)S(1)}, u32[]{:S(2)}, u32[]{:S(2)}) %all-to-all-start.1) | async-done | bytes 1048608 | tf_op jit(solution)/shard_map/while/body/eval_jaxpr/all_to_all | solution.py:66
  508.8 9.8 %collective-permute-done = bf16[32,4096]{1,0:T(8,128)(2,1)S(1)} collective-permute-done((bf16[32,4096]{1,0:T(8,128)(2,1)S(1)}, bf16[32,4096]{1,0:T(8,128)(2,1)S(1)}, u32[]{:S(2)}, u32[]{:S(2)}) %collective-permute-start) | collective-permute-done | bytes 262176 | tf_op jit(solution)/shard_map/while/body/eval_jaxpr/ppermute | solution.py:12
  526.4 16.8 %all-to-all-done = bf16[32,4,4096]{2,1,0:T(4,128)(2,1)S(1)} async-done(((bf16[32,4,4096]{2,1,0:T(4,128)(2,1)}), bf16[32,4,4096]{2,1,0:T(4,128)(2,1)S(1)}, u32[]{:S(2)}, u32[]{:S(2)}) %all-to-all-start) | async-done | bytes 1048608 | tf_op jit(solution)/shard_map/while/body/eval_jaxpr/all_to_all | solution.py:56
  556.3 16.1 %all-to-all-done.1 = bf16[32,4,4096]{2,1,0:T(4,128)(2,1)S(1)} async-done(((bf16[32,4,4096]{2,1,0:T(4,128)(2,1)}), bf16[32,4,4096]{2,1,0:T(4,128)(2,1)S(1)}, u32[]{:S(2)}, u32[]{:S(2)}) %all-to-all-start.1) | async-done | bytes 1048608 | tf_op jit(solution)/shard_map/while/body/eval_jaxpr/all_to_all | solution.py:66
  573.3 9.8 %collective-permute-done = bf16[32,4096]{1,0:T(8,128)(2,1)S(1)} collective-permute-done((bf16[32,4096]{1,0:T(8,128)(2,1)S(1)}, bf16[32,4096]{1,0:T(8,128)(2,1)S(1)}, u32[]{:S(2)}, u32[]{:S(2)}) %collective-permute-start) | collective-permute-done | bytes 262176 | tf_op jit(solution)/shard_map/while/body/eval_jaxpr/ppermute | solution.py:12
  590.8 16.8 %all-to-all-done = bf16[32,4,4096]{2,1,0:T(4,128)(2,1)S(1)} async-done(((bf16[32,4,4096]{2,1,0:T(4,128)(2,1)}), bf16[32,4,4096]{2,1,0:T(4,128)(2,1)S(1)}, u32[]{:S(2)}, u32[]{:S(2)}) %all-to-all-start) | async-done | bytes 1048608 | tf_op jit(solution)/shard_map/while/body/eval_jaxpr/all_to_all | solution.py:56
  620.7 16.1 %all-to-all-done.1 = bf16[32,4,4096]{2,1,0:T(4,128)(2,1)S(1)} async-done(((bf16[32,4,4096]{2,1,0:T(4,128)(2,1)}), bf16[32,4,4096]{2,1,0:T(4,128)(2,1)S(1)}, u32[]{:S(2)}, u32[]{:S(2)}) %all-to-all-start.1) | async-done | bytes 1048608 | tf_op jit(solution)/shard_map/while/body/eval_jaxpr/all_to_all | solution.py:66
  637.7 9.8 %collective-permute-done = bf16[32,4096]{1,0:T(8,128)(2,1)S(1)} collective-permute-done((bf16[32,4096]{1,0:T(8,128)(2,1)S(1)}, bf16[32,4096]{1,0:T(8,128)(2,1)S(1)}, u32[]{:S(2)}, u32[]{:S(2)}) %collective-permute-start) | collective-permute-done | bytes 262176 | tf_op jit(solution)/shard_map/while/body/eval_jaxpr/ppermute | solution.py:12
  655.3 16.8 %all-to-all-done = bf16[32,4,4096]{2,1,0:T(4,128)(2,1)S(1)} async-done(((bf16[32,4,4096]{2,1,0:T(4,128)(2,1)}), bf16[32,4,4096]{2,1,0:T(4,128)(2,1)S(1)}, u32[]{:S(2)}, u32[]{:S(2)}) %all-to-all-start) | async-done | bytes 1048608 | tf_op jit(solution)/shard_map/while/body/eval_jaxpr/all_to_all | solution.py:56
  685.2 16.1 %all-to-all-done.1 = bf16[32,4,4096]{2,1,0:T(4,128)(2,1)S(1)} async-done(((bf16[32,4,4096]{2,1,0:T(4,128)(2,1)}), bf16[32,4,4096]{2,1,0:T(4,128)(2,1)S(1)}, u32[]{:S(2)}, u32[]{:S(2)}) %all-to-all-start.1) | async-done | bytes 1048608 | tf_op jit(solution)/shard_map/while/body/eval_jaxpr/all_to_all | solution.py:66
  702.2 9.8 %collective-permute-done = bf16[32,4096]{1,0:T(8,128)(2,1)S(1)} collective-permute-done((bf16[32,4096]{1,0:T(8,128)(2,1)S(1)}, bf16[32,4096]{1,0:T(8,128)(2,1)S(1)}, u32[]{:S(2)}, u32[]{:S(2)}) %collective-permute-start) | collective-permute-done | bytes 262176 | tf_op jit(solution)/shard_map/while/body/eval_jaxpr/ppermute | solution.py:12
  712.0 9.0 %collective-permute-done.1 = bf16[32,4096]{1,0:T(8,128)(2,1)S(1)} collective-permute-done((bf16[32,4096]{1,0:T(8,128)(2,1)S(1)}, bf16[32,4096]{1,0:T(8,128)(2,1)S(1)}, u32[]{:S(2)}, u32[]{:S(2)}) %collective-permute-start.1) | collective-permute-done | bytes 262176 | tf_op jit(solution)/shard_map/ppermute | solution.py:12
  (270 shorter events, 272.1 us)
Async XLA Ops:
  4.8 25.0 %all-to-all-start = ((bf16[32,4,4096]{2,1,0:T(4,128)(2,1)}), bf16[32,4,4096]{2,1,0:T(4,128)(2,1)S(1)}, u32[]{:S(2)}, u32[]{:S(2)}) async-start(bf16[32,4,4096]{2,1,0:T(4,128)(2,1)} %bitcast.62), calls=%async_computation | async-start | bytes 2097152 | tf_op jit(solution)/shard_map/while/body/eval_jaxpr/all_to_all | solution.py:56
  38.1 20.9 %all-to-all-start.1 = ((bf16[32,4,4096]{2,1,0:T(4,128)(2,1)}), bf16[32,4,4096]{2,1,0:T(4,128)(2,1)S(1)}, u32[]{:S(2)}, u32[]{:S(2)}) async-start(bf16[32,4,4096]{2,1,0:T(4,128)(2,1)} %reshape.87), calls=%async_computation.1 | async-start | bytes 2097152 | tf_op jit(solution)/shard_map/while/body/eval_jaxpr/all_to_all | solution.py:66
  72.3 20.7 %all-to-all-start = ((bf16[32,4,4096]{2,1,0:T(4,128)(2,1)}), bf16[32,4,4096]{2,1,0:T(4,128)(2,1)S(1)}, u32[]{:S(2)}, u32[]{:S(2)}) async-start(bf16[32,4,4096]{2,1,0:T(4,128)(2,1)} %bitcast.62), calls=%async_computation | async-start | bytes 2097152 | tf_op jit(solution)/shard_map/while/body/eval_jaxpr/all_to_all | solution.py:56
  101.4 20.9 %all-to-all-start.1 = ((bf16[32,4,4096]{2,1,0:T(4,128)(2,1)}), bf16[32,4,4096]{2,1,0:T(4,128)(2,1)S(1)}, u32[]{:S(2)}, u32[]{:S(2)}) async-start(bf16[32,4,4096]{2,1,0:T(4,128)(2,1)} %reshape.87), calls=%async_computation.1 | async-start | bytes 2097152 | tf_op jit(solution)/shard_map/while/body/eval_jaxpr/all_to_all | solution.py:66
  135.6 20.7 %all-to-all-start = ((bf16[32,4,4096]{2,1,0:T(4,128)(2,1)}), bf16[32,4,4096]{2,1,0:T(4,128)(2,1)S(1)}, u32[]{:S(2)}, u32[]{:S(2)}) async-start(bf16[32,4,4096]{2,1,0:T(4,128)(2,1)} %bitcast.62), calls=%async_computation | async-start | bytes 2097152 | tf_op jit(solution)/shard_map/while/body/eval_jaxpr/all_to_all | solution.py:56
  164.7 20.9 %all-to-all-start.1 = ((bf16[32,4,4096]{2,1,0:T(4,128)(2,1)}), bf16[32,4,4096]{2,1,0:T(4,128)(2,1)S(1)}, u32[]{:S(2)}, u32[]{:S(2)}) async-start(bf16[32,4,4096]{2,1,0:T(4,128)(2,1)} %reshape.87), calls=%async_computation.1 | async-start | bytes 2097152 | tf_op jit(solution)/shard_map/while/body/eval_jaxpr/all_to_all | solution.py:66
  186.3 9.8 %collective-permute-start = (bf16[32,4096]{1,0:T(8,128)(2,1)S(1)}, bf16[32,4096]{1,0:T(8,128)(2,1)S(1)}, u32[]{:S(2)}, u32[]{:S(2)}) collective-permute-start(bf16[32,4096]{1,0:T(8,128)(2,1)S(1)} %fusion.62), channel_id=1, source_target_pairs={{0,32},{32,64},{64,96},{96,0},{1,33},{33,65},{65,97},{97,1},{2,34}... | collective-permute-start | bytes 786440 | tf_op jit(solution)/shard_map/while/body/eval_jaxpr/ppermute | solution.py:12
  200.0 20.7 %all-to-all-start = ((bf16[32,4,4096]{2,1,0:T(4,128)(2,1)}), bf16[32,4,4096]{2,1,0:T(4,128)(2,1)S(1)}, u32[]{:S(2)}, u32[]{:S(2)}) async-start(bf16[32,4,4096]{2,1,0:T(4,128)(2,1)} %bitcast.62), calls=%async_computation | async-start | bytes 2097152 | tf_op jit(solution)/shard_map/while/body/eval_jaxpr/all_to_all | solution.py:56
  229.1 20.9 %all-to-all-start.1 = ((bf16[32,4,4096]{2,1,0:T(4,128)(2,1)}), bf16[32,4,4096]{2,1,0:T(4,128)(2,1)S(1)}, u32[]{:S(2)}, u32[]{:S(2)}) async-start(bf16[32,4,4096]{2,1,0:T(4,128)(2,1)} %reshape.87), calls=%async_computation.1 | async-start | bytes 2097152 | tf_op jit(solution)/shard_map/while/body/eval_jaxpr/all_to_all | solution.py:66
  250.8 9.9 %collective-permute-start = (bf16[32,4096]{1,0:T(8,128)(2,1)S(1)}, bf16[32,4096]{1,0:T(8,128)(2,1)S(1)}, u32[]{:S(2)}, u32[]{:S(2)}) collective-permute-start(bf16[32,4096]{1,0:T(8,128)(2,1)S(1)} %fusion.62), channel_id=1, source_target_pairs={{0,32},{32,64},{64,96},{96,0},{1,33},{33,65},{65,97},{97,1},{2,34}... | collective-permute-start | bytes 786440 | tf_op jit(solution)/shard_map/while/body/eval_jaxpr/ppermute | solution.py:12
  264.5 20.7 %all-to-all-start = ((bf16[32,4,4096]{2,1,0:T(4,128)(2,1)}), bf16[32,4,4096]{2,1,0:T(4,128)(2,1)S(1)}, u32[]{:S(2)}, u32[]{:S(2)}) async-start(bf16[32,4,4096]{2,1,0:T(4,128)(2,1)} %bitcast.62), calls=%async_computation | async-start | bytes 2097152 | tf_op jit(solution)/shard_map/while/body/eval_jaxpr/all_to_all | solution.py:56
  293.6 20.9 %all-to-all-start.1 = ((bf16[32,4,4096]{2,1,0:T(4,128)(2,1)}), bf16[32,4,4096]{2,1,0:T(4,128)(2,1)S(1)}, u32[]{:S(2)}, u32[]{:S(2)}) async-start(bf16[32,4,4096]{2,1,0:T(4,128)(2,1)} %reshape.87), calls=%async_computation.1 | async-start | bytes 2097152 | tf_op jit(solution)/shard_map/while/body/eval_jaxpr/all_to_all | solution.py:66
  315.3 9.9 %collective-permute-start = (bf16[32,4096]{1,0:T(8,128)(2,1)S(1)}, bf16[32,4096]{1,0:T(8,128)(2,1)S(1)}, u32[]{:S(2)}, u32[]{:S(2)}) collective-permute-start(bf16[32,4096]{1,0:T(8,128)(2,1)S(1)} %fusion.62), channel_id=1, source_target_pairs={{0,32},{32,64},{64,96},{96,0},{1,33},{33,65},{65,97},{97,1},{2,34}... | collective-permute-start | bytes 786440 | tf_op jit(solution)/shard_map/while/body/eval_jaxpr/ppermute | solution.py:12
  329.0 20.7 %all-to-all-start = ((bf16[32,4,4096]{2,1,0:T(4,128)(2,1)}), bf16[32,4,4096]{2,1,0:T(4,128)(2,1)S(1)}, u32[]{:S(2)}, u32[]{:S(2)}) async-start(bf16[32,4,4096]{2,1,0:T(4,128)(2,1)} %bitcast.62), calls=%async_computation | async-start | bytes 2097152 | tf_op jit(solution)/shard_map/while/body/eval_jaxpr/all_to_all | solution.py:56
  358.1 20.9 %all-to-all-start.1 = ((bf16[32,4,4096]{2,1,0:T(4,128)(2,1)}), bf16[32,4,4096]{2,1,0:T(4,128)(2,1)S(1)}, u32[]{:S(2)}, u32[]{:S(2)}) async-start(bf16[32,4,4096]{2,1,0:T(4,128)(2,1)} %reshape.87), calls=%async_computation.1 | async-start | bytes 2097152 | tf_op jit(solution)/shard_map/while/body/eval_jaxpr/all_to_all | solution.py:66
  379.8 9.9 %collective-permute-start = (bf16[32,4096]{1,0:T(8,128)(2,1)S(1)}, bf16[32,4096]{1,0:T(8,128)(2,1)S(1)}, u32[]{:S(2)}, u32[]{:S(2)}) collective-permute-start(bf16[32,4096]{1,0:T(8,128)(2,1)S(1)} %fusion.62), channel_id=1, source_target_pairs={{0,32},{32,64},{64,96},{96,0},{1,33},{33,65},{65,97},{97,1},{2,34}... | collective-permute-start | bytes 786440 | tf_op jit(solution)/shard_map/while/body/eval_jaxpr/ppermute | solution.py:12
  393.5 20.7 %all-to-all-start = ((bf16[32,4,4096]{2,1,0:T(4,128)(2,1)}), bf16[32,4,4096]{2,1,0:T(4,128)(2,1)S(1)}, u32[]{:S(2)}, u32[]{:S(2)}) async-start(bf16[32,4,4096]{2,1,0:T(4,128)(2,1)} %bitcast.62), calls=%async_computation | async-start | bytes 2097152 | tf_op jit(solution)/shard_map/while/body/eval_jaxpr/all_to_all | solution.py:56
  422.6 20.9 %all-to-all-start.1 = ((bf16[32,4,4096]{2,1,0:T(4,128)(2,1)}), bf16[32,4,4096]{2,1,0:T(4,128)(2,1)S(1)}, u32[]{:S(2)}, u32[]{:S(2)}) async-start(bf16[32,4,4096]{2,1,0:T(4,128)(2,1)} %reshape.87), calls=%async_computation.1 | async-start | bytes 2097152 | tf_op jit(solution)/shard_map/while/body/eval_jaxpr/all_to_all | solution.py:66
  444.2 9.9 %collective-permute-start = (bf16[32,4096]{1,0:T(8,128)(2,1)S(1)}, bf16[32,4096]{1,0:T(8,128)(2,1)S(1)}, u32[]{:S(2)}, u32[]{:S(2)}) collective-permute-start(bf16[32,4096]{1,0:T(8,128)(2,1)S(1)} %fusion.62), channel_id=1, source_target_pairs={{0,32},{32,64},{64,96},{96,0},{1,33},{33,65},{65,97},{97,1},{2,34}... | collective-permute-start | bytes 786440 | tf_op jit(solution)/shard_map/while/body/eval_jaxpr/ppermute | solution.py:12
  458.0 20.7 %all-to-all-start = ((bf16[32,4,4096]{2,1,0:T(4,128)(2,1)}), bf16[32,4,4096]{2,1,0:T(4,128)(2,1)S(1)}, u32[]{:S(2)}, u32[]{:S(2)}) async-start(bf16[32,4,4096]{2,1,0:T(4,128)(2,1)} %bitcast.62), calls=%async_computation | async-start | bytes 2097152 | tf_op jit(solution)/shard_map/while/body/eval_jaxpr/all_to_all | solution.py:56
  487.0 20.9 %all-to-all-start.1 = ((bf16[32,4,4096]{2,1,0:T(4,128)(2,1)}), bf16[32,4,4096]{2,1,0:T(4,128)(2,1)S(1)}, u32[]{:S(2)}, u32[]{:S(2)}) async-start(bf16[32,4,4096]{2,1,0:T(4,128)(2,1)} %reshape.87), calls=%async_computation.1 | async-start | bytes 2097152 | tf_op jit(solution)/shard_map/while/body/eval_jaxpr/all_to_all | solution.py:66
  508.7 9.9 %collective-permute-start = (bf16[32,4096]{1,0:T(8,128)(2,1)S(1)}, bf16[32,4096]{1,0:T(8,128)(2,1)S(1)}, u32[]{:S(2)}, u32[]{:S(2)}) collective-permute-start(bf16[32,4096]{1,0:T(8,128)(2,1)S(1)} %fusion.62), channel_id=1, source_target_pairs={{0,32},{32,64},{64,96},{96,0},{1,33},{33,65},{65,97},{97,1},{2,34}... | collective-permute-start | bytes 786440 | tf_op jit(solution)/shard_map/while/body/eval_jaxpr/ppermute | solution.py:12
  522.4 20.7 %all-to-all-start = ((bf16[32,4,4096]{2,1,0:T(4,128)(2,1)}), bf16[32,4,4096]{2,1,0:T(4,128)(2,1)S(1)}, u32[]{:S(2)}, u32[]{:S(2)}) async-start(bf16[32,4,4096]{2,1,0:T(4,128)(2,1)} %bitcast.62), calls=%async_computation | async-start | bytes 2097152 | tf_op jit(solution)/shard_map/while/body/eval_jaxpr/all_to_all | solution.py:56
  551.5 20.9 %all-to-all-start.1 = ((bf16[32,4,4096]{2,1,0:T(4,128)(2,1)}), bf16[32,4,4096]{2,1,0:T(4,128)(2,1)S(1)}, u32[]{:S(2)}, u32[]{:S(2)}) async-start(bf16[32,4,4096]{2,1,0:T(4,128)(2,1)} %reshape.87), calls=%async_computation.1 | async-start | bytes 2097152 | tf_op jit(solution)/shard_map/while/body/eval_jaxpr/all_to_all | solution.py:66
  573.2 9.9 %collective-permute-start = (bf16[32,4096]{1,0:T(8,128)(2,1)S(1)}, bf16[32,4096]{1,0:T(8,128)(2,1)S(1)}, u32[]{:S(2)}, u32[]{:S(2)}) collective-permute-start(bf16[32,4096]{1,0:T(8,128)(2,1)S(1)} %fusion.62), channel_id=1, source_target_pairs={{0,32},{32,64},{64,96},{96,0},{1,33},{33,65},{65,97},{97,1},{2,34}... | collective-permute-start | bytes 786440 | tf_op jit(solution)/shard_map/while/body/eval_jaxpr/ppermute | solution.py:12
  586.9 20.7 %all-to-all-start = ((bf16[32,4,4096]{2,1,0:T(4,128)(2,1)}), bf16[32,4,4096]{2,1,0:T(4,128)(2,1)S(1)}, u32[]{:S(2)}, u32[]{:S(2)}) async-start(bf16[32,4,4096]{2,1,0:T(4,128)(2,1)} %bitcast.62), calls=%async_computation | async-start | bytes 2097152 | tf_op jit(solution)/shard_map/while/body/eval_jaxpr/all_to_all | solution.py:56
  616.0 20.9 %all-to-all-start.1 = ((bf16[32,4,4096]{2,1,0:T(4,128)(2,1)}), bf16[32,4,4096]{2,1,0:T(4,128)(2,1)S(1)}, u32[]{:S(2)}, u32[]{:S(2)}) async-start(bf16[32,4,4096]{2,1,0:T(4,128)(2,1)} %reshape.87), calls=%async_computation.1 | async-start | bytes 2097152 | tf_op jit(solution)/shard_map/while/body/eval_jaxpr/all_to_all | solution.py:66
  637.7 9.9 %collective-permute-start = (bf16[32,4096]{1,0:T(8,128)(2,1)S(1)}, bf16[32,4096]{1,0:T(8,128)(2,1)S(1)}, u32[]{:S(2)}, u32[]{:S(2)}) collective-permute-start(bf16[32,4096]{1,0:T(8,128)(2,1)S(1)} %fusion.62), channel_id=1, source_target_pairs={{0,32},{32,64},{64,96},{96,0},{1,33},{33,65},{65,97},{97,1},{2,34}... | collective-permute-start | bytes 786440 | tf_op jit(solution)/shard_map/while/body/eval_jaxpr/ppermute | solution.py:12
  651.4 20.7 %all-to-all-start = ((bf16[32,4,4096]{2,1,0:T(4,128)(2,1)}), bf16[32,4,4096]{2,1,0:T(4,128)(2,1)S(1)}, u32[]{:S(2)}, u32[]{:S(2)}) async-start(bf16[32,4,4096]{2,1,0:T(4,128)(2,1)} %bitcast.62), calls=%async_computation | async-start | bytes 2097152 | tf_op jit(solution)/shard_map/while/body/eval_jaxpr/all_to_all | solution.py:56
  680.5 20.9 %all-to-all-start.1 = ((bf16[32,4,4096]{2,1,0:T(4,128)(2,1)}), bf16[32,4,4096]{2,1,0:T(4,128)(2,1)S(1)}, u32[]{:S(2)}, u32[]{:S(2)}) async-start(bf16[32,4,4096]{2,1,0:T(4,128)(2,1)} %reshape.87), calls=%async_computation.1 | async-start | bytes 2097152 | tf_op jit(solution)/shard_map/while/body/eval_jaxpr/all_to_all | solution.py:66
  702.1 9.9 %collective-permute-start = (bf16[32,4096]{1,0:T(8,128)(2,1)S(1)}, bf16[32,4096]{1,0:T(8,128)(2,1)S(1)}, u32[]{:S(2)}, u32[]{:S(2)}) collective-permute-start(bf16[32,4096]{1,0:T(8,128)(2,1)S(1)} %fusion.62), channel_id=1, source_target_pairs={{0,32},{32,64},{64,96},{96,0},{1,33},{33,65},{65,97},{97,1},{2,34}... | collective-permute-start | bytes 786440 | tf_op jit(solution)/shard_map/while/body/eval_jaxpr/ppermute | solution.py:12
  712.0 9.0 %collective-permute-start.1 = (bf16[32,4096]{1,0:T(8,128)(2,1)S(1)}, bf16[32,4096]{1,0:T(8,128)(2,1)S(1)}, u32[]{:S(2)}, u32[]{:S(2)}) collective-permute-start(bf16[32,4096]{1,0:T(8,128)(2,1)S(1)} %get-tuple-element.234), channel_id=1, source_target_pairs={{0,32},{32,64},{64,96},{96,0},{1,33},{33,65},{65,97},{97,1},{2,34}... | collective-permute-start | bytes 786440 | tf_op jit(solution)/shard_map/ppermute | solution.py:12
  (2 other events, 17.3 us)
where the time goes:
time: 728 us; the launch traced here: 722 us
  waiting for transfers between devices  471 us (65%)
  starting transfers between devices  97.9 us (13%)
  matrix products  81.5 us (11%)
  local copies, waits for them, and re-layouts  61.8 us (8%)
  other arithmetic  8.71 us (1%)
    all_to_all x11, waiting for transfers between devices, run_layer(): lax.all_to_all(outgoing, 'expert', split_axis=0, concat_axis=0, tiled=True)  185 us
    all_to_all x11, waiting for transfers between devices, run_layer(): lax.all_to_all(partial_out, 'expert', split_axis=0, concat_axis=0, tiled=...  177 us
    ppermute x12, waiting for transfers between devices, from_behind(): return lax.ppermute(x, axis, [(i, (i + by) % count) for i in range(count)])  109 us
    all_to_all x11, starting transfers between devices, run_layer(): lax.all_to_all(outgoing, 'expert', split_axis=0, concat_axis=0, tiled=True)  47.5 us
    dot_general x11, matrix products, run_layer(): jnp.dot(hidden, weight_down, preferred_element_type=jnp.float32)  46.6 us
    all_to_all x11, starting transfers between devices, run_layer(): lax.all_to_all(partial_out, 'expert', split_axis=0, concat_axis=0, tiled=...  44.4 us
    dot_general x11, matrix products, run_layer(): gate = jnp.dot(flat, weight_in[0], preferred_element_type=jnp.float32)  28.7 us
    broadcast_in_dim x11, local copies, waits for them, and re-layouts, run_layer(): jnp.broadcast_to(packed[:, None], (n_window, SPLIT, capacity, width))  16.7 us
  transfers between devices with their start and end apart: 34, of which 34 were waited for; matrix products, arithmetic and copies ran while one was open for 1% of the time, Pallas kernels for 0%

commit v1 on v0

v1 whole, which is shorter than its diff:
```python
import functools

import jax
import jax.numpy as jnp
from jax import lax
from jax.experimental import pallas as pl
from jax.experimental.pallas import tpu as pltpu
from jax.sharding import Mesh
from jax.sharding import PartitionSpec as P

SPLIT = 4
CAP = 4
CHIPS = ("x", "z")
SWAP = [(0, 1), (1, 0)]

IN_VMEM = pl.BlockSpec(memory_space=pltpu.VMEM)
IN_SMEM = pl.BlockSpec(memory_space=pltpu.SMEM)
IN_HBM = pl.BlockSpec(memory_space=pltpu.HBM)
MIB = 2**20
EARLY = ((0,), (1,), (2, 3))


def dot(a, b):
    return jnp.dot(a, b, preferred_element_type=jnp.float32)


def dot_first(a, b):
    return lax.dot_general(a, b, (((0,), (0,)), ((), ())), preferred_element_type=jnp.float32)


def as_bf16(mask):
    return mask.astype(jnp.float32).astype(jnp.bfloat16)


def schedule(step, section, sections, layers):
    micro = lax.rem(section[0] - step + 16 * sections, sections)
    level = step - lax.rem(sections - micro, sections)
    active = jnp.logical_and(level >= 0, level < layers)
    repeat = jnp.where(level >= sections, 1, 0)
    return repeat, repeat * sections + micro, active


def table_kernel(ids, gates, hot, mix):
    groups, rows, topk = ids.shape
    wide = hot.shape[2]
    column = lax.broadcasted_iota(jnp.int32, (rows, wide), 1)
    expert = column // (2 * CAP * (SPLIT // 2))
    slot = column - column // CAP * CAP
    half = column // CAP - column // (2 * CAP) * 2
    earlier = as_bf16(lax.broadcasted_iota(jnp.int32, (rows, rows), 0) > lax.broadcasted_iota(jnp.int32, (rows, rows), 1))
    for group in range(groups):
        chosen = jnp.zeros((rows, wide), jnp.float32)
        weight = jnp.zeros((rows, wide), jnp.float32)
        for k in range(topk):
            match = ids[group, :, k : k + 1] == expert
            chosen = jnp.where(match, 1.0, chosen)
            weight = jnp.where(match, weight + gates[group, :, k : k + 1], weight)
        position = dot(earlier, chosen.astype(jnp.bfloat16))
        taken = jnp.where(position == slot.astype(jnp.float32), chosen, 0.0)
        for k in range(2):
            here = jnp.where(half == k, taken, 0.0)
            scaled = here * weight
            high = scaled.astype(jnp.bfloat16)
            hot[group, k * rows : (k + 1) * rows, :] = here.astype(jnp.bfloat16)
            mix[0, group, k * rows : (k + 1) * rows, :] = high
            mix[1, group, k * rows : (k + 1) * rows, :] = (scaled - high.astype(jnp.float32)).astype(jnp.bfloat16)


def pack_kernel(when, section, x, gain, hot, out):
    repeat, group, _ = when(section)
    values = x[...].astype(jnp.float32)
    scale = lax.rsqrt(jnp.mean(values * values, axis=-1, keepdims=True) + 1e-06)
    normed = (values * scale * gain[pl.ds(repeat, 1), :]).astype(jnp.bfloat16)
    half = normed.shape[1] // 2
    stacked = jnp.concatenate([normed[:, :half], normed[:, half:]], axis=0)
    out[...] = dot_first(hot[group], stacked).astype(jnp.bfloat16)


def place(rows, columns, offset, transposed):
    shape = (columns, rows) if transposed else (rows, columns)
    row = lax.broadcasted_iota(jnp.int32, shape, int(transposed))
    column = lax.broadcasted_iota(jnp.int32, shape, 1 - int(transposed))
    block = column // (2 * CAP)
    inner = column - block * (2 * CAP) - offset
    return as_bf16((block * CAP + inner == row) & (inner >= 0) & (inner < CAP))


def gather_rows(rows, x):
    wide, half = rows.shape
    got = rows[...]
    for k in range(2):
        x[:, k * half : (k + 1) * half] = dot(place(wide // 2, wide, k * CAP, False), got).astype(jnp.bfloat16)


def hidden_rows(x, w_in):
    given = x[...]
    count = given.shape[0]
    gate = dot(given, w_in[0])
    upward = dot(given, w_in[1])
    part = (gate / (1.0 + jnp.exp(-gate)) * upward).astype(jnp.bfloat16)
    return [dot(place(count, 2 * count, k * CAP, True), part).astype(jnp.bfloat16) for k in range(2)]


def down_rows(hidden, downs, out):
    half = out.shape[1]
    pieces = 4
    size = half // pieces
    for j in range(pieces):
        total = None
        for k in range(2):
            for spread, w_down in zip(hidden, downs):
                partial = dot(spread[k], w_down[:, k * half + j * size : k * half + (j + 1) * size])
                total = partial if total is None else total + partial
        out[:, j * size : (j + 1) * size] = total.astype(jnp.bfloat16)


def experts(rows, x, held, repeat, out):
    gather_rows(rows, x)
    hidden = [hidden_rows(x, w.at[repeat]) for w in held[:2]]
    down_rows(hidden, [w.at[repeat] for w in held[2:]], out)


def first_expert_kernel(rows, *refs):
    given, out, held, (x, sems) = refs[:4], refs[4], refs[5:9], refs[9:]
    copies = [
        pltpu.make_async_copy(source.at[0, 0], to.at[0], sems.at[k]) for k, (source, to) in enumerate(zip(given, held))
    ]
    for copy in copies:
        copy.start()
    gather_rows(rows, x)
    hidden = []
    for k in range(2):
        copies[k].wait()
        hidden.append(hidden_rows(x, held[k].at[0]))
    for copy in copies[2:]:
        copy.wait()
    down_rows(hidden, [w.at[0] for w in held[2:]], out)


def early_expert_kernel(parts, rows, *refs):
    given, refs = refs[: len(parts)], refs[len(parts) :]
    held, out, after, (x, sems) = refs[:4], refs[4], refs[5:9], refs[9:]
    copies = [
        pltpu.make_async_copy(source.at[1, 0], after[k].at[1], sems.at[n]) for n, (source, k) in enumerate(zip(given, parts))
    ]
    for copy in copies:
        copy.start()
    experts(rows, x, held, 0, out)
    for copy in copies:
        copy.wait()


def expert_kernel(when, section, rows, *refs):
    repeat, _, _ = when(section)
    experts(rows, refs[-1], refs[:4], repeat, refs[4])


def mix_kernel(when, section, x, returned, mix, out):
    _, group, active = when(section)
    got = returned[...]
    update = dot(mix[0, group], got) + dot(mix[1, group], got)
    rows = x.shape[0]
    update = jnp.concatenate([update[:rows], update[rows:]], axis=1)
    values = x[...].astype(jnp.float32)
    out[...] = jnp.where(active, values + update, values).astype(jnp.bfloat16)


def kernel(name, function, out_shape, in_specs, limit=4, scratch=(), aliases=None):
    return pl.pallas_call(
        function,
        out_shape=out_shape,
        in_specs=in_specs,
        out_specs=jax.tree.map(lambda _: IN_VMEM, out_shape),
        scratch_shapes=list(scratch),
        input_output_aliases=aliases or {},
        compiler_params=pltpu.CompilerParams(vmem_limit_bytes=limit * MIB),
        name=name,
    )


def body(tokens, w_in, w_down, norm_gain, route_ids, gate_values):
    sections = lax.axis_size("section")
    chips = lax.axis_size("x") * lax.axis_size("z")
    repeats, _, micros, rows, topk = route_ids.shape
    layers = repeats * sections
    steps = layers + sections - 1
    groups = repeats * micros
    section = lax.axis_index("section").astype(jnp.int32).reshape(1)
    width = tokens.shape[-1]
    slots = chips * 2 * CAP
    bf16 = lambda *shape: jax.ShapeDtypeStruct(shape, jnp.bfloat16)

    hot, mix = kernel(
        "tables", table_kernel, (bf16(groups, 2 * rows, slots), bf16(2, groups, 2 * rows, slots)), [IN_VMEM] * 2
    )(route_ids.reshape(groups, rows, topk), gate_values.reshape(groups, rows, topk))
    gain = norm_gain.reshape(repeats, width)

    def kept(*arrays):
        return [pltpu.with_memory_space_constraint(a, pltpu.VMEM) for a in arrays]

    def outside(*arrays):
        return [pltpu.with_memory_space_constraint(a, pltpu.HBM) for a in arrays]

    given = (w_in, lax.ppermute(w_in, "core", SWAP), w_down, lax.ppermute(w_down, "core", SWAP))
    held = tuple(pltpu.VMEM((repeats,) + w.shape[2:], jnp.bfloat16) for w in given)
    wide = bf16(slots, width // 2)

    def across(v):
        v = v.reshape(chips, 2 * CAP, width // 2)
        v = lax.all_to_all(v, CHIPS, split_axis=0, concat_axis=0, tiled=True)
        return v.reshape(slots, width // 2)

    def relay(v, by):
        return lax.ppermute(v, "section", [(i, (i + by) % sections) for i in range(sections)])

    state = tokens[0]
    for step in range(steps):
        when = functools.partial(schedule, step, sections=sections, layers=layers)
        packed = kernel("norm_pack", functools.partial(pack_kernel, when), wide, [IN_SMEM] + [IN_VMEM] * 3)(
            section, state, gain, hot
        )
        arrived = across(packed)
        x = pltpu.VMEM((slots // 2, width), jnp.bfloat16)
        if step == 0:
            outputs, *weights = kernel(
                "first_experts",
                first_expert_kernel,
                (wide, *held),
                [IN_VMEM] + [IN_HBM] * 4,
                scratch=[x, pltpu.SemaphoreType.DMA((4,))],
            )(arrived, *outside(*given))
        elif step <= len(EARLY):
            parts = EARLY[step - 1]
            outputs, *weights = kernel(
                "early_experts",
                functools.partial(early_expert_kernel, parts),
                (wide, *held),
                [IN_VMEM] + [IN_HBM] * len(parts) + [IN_VMEM] * 4,
                scratch=[x, pltpu.SemaphoreType.DMA((2,))],
                aliases={1 + len(parts) + k: 1 + k for k in range(4)},
            )(arrived, *outside(*(given[k] for k in parts)), *kept(*weights))
        else:
            outputs, *weights = kernel(
                "experts",
                functools.partial(expert_kernel, when),
                (wide, *held),
                [IN_SMEM] + [IN_VMEM] * 5,
                scratch=[x],
                aliases={2 + k: 1 + k for k in range(4)},
            )(section, arrived, *kept(*weights))
        returned = across(outputs)
        mixed = kernel("mix", functools.partial(mix_kernel, when), bf16(rows, width), [IN_SMEM] + [IN_VMEM] * 3)(
            section, state, returned, mix
        )
        if step < steps - 1:
            state = relay(mixed, 1)
    waiting = relay(state, 2)
    last = lax.ppermute(mixed, "section", [(sections - 1, 1)])
    return jnp.where(section[0] == 1, last, waiting)[None]


def solution(mesh):
    fine = Mesh(mesh.devices.reshape(4, 4, 4, 2), ("section", "x", "z", "core"))
    expert = ("x", "z", "core")
    return jax.shard_map(
        body,
        mesh=fine,
        in_specs=(
            P("section", expert, None),
            P(None, "section", None, None, expert),
            P(None, "section", expert, None),
            P(None, "section", None),
            P(None, "section", None, expert, None),
            P(None, "section", None, expert, None),
        ),
        out_specs=P("section", expert, None),
        check_vma=False,
    )
```

time: 728 us -> 473 us (0.65)
  waiting for transfers between devices: 471 us -> 90.4 us
  blocking collectives: 0 us -> 300 us
  starting transfers between devices: 97.9 us -> 13.2 us
  matrix products: 81.5 us -> 0 us
  local copies, waits for them, and re-layouts: 61.8 us -> 3.43 us
  Pallas kernels: 0 us -> 55.2 us
  other arithmetic: 8.71 us -> 0.73 us
    all_to_all x22 -> x1, waiting for transfers between devices: 362 us -> 8.37 us  [across(): v = lax.all_to_all(v, CHIPS, split_axis=0, concat_axis=0, tiled=True)]
    all_to_all x0 -> x21, blocking collectives: none -> 300 us  [across(): v = lax.all_to_all(v, CHIPS, split_axis=0, concat_axis=0, tiled=True)]
    all_to_all x22 -> x1, starting transfers between devices: 91.9 us -> 3.57 us  [across(): v = lax.all_to_all(v, CHIPS, split_axis=0, concat_axis=0, tiled=True)]
    dot_general x44 -> x0, matrix products: 81.5 us -> none  [the longest x11 46.6 us: run_layer(): jnp.dot(hidden, weight_down, preferred_element_type=jnp.float32)]
    pallas_call x0 -> x34, Pallas kernels: none -> 55.2 us  [the longest x7 27.3 us: body(): kernel('experts', functools.partial(expert_kernel, when), (wide, *held),...]
    ppermute x12 -> x14, waiting for transfers between devices: 109 us -> 82 us  [the longest x11 69.6 us: relay(): lax.ppermute(v, 'section', [(i, (i + by) % sections) for i in range(secti...]
    broadcast_in_dim x22 -> x0, local copies, waits for them, and re-layouts: 24.3 us -> none  [the longest x11 16.7 us: run_layer(): jnp.broadcast_to(packed[:, None], (n_window, SPLIT, capacity, width))]
    reshape x22 -> x0, local copies, waits for them, and re-layouts: 16.4 us -> none  [the longest x11 13.5 us: run_layer(): partial_out = partial_out.reshape(members, count, width)]
  transfers between devices with their start and end apart: 34 -> 15, of which waited for: 34 -> 13; matrix products, arithmetic and copies ran while one was open for 1% -> 1% of each run, Pallas kernels for 0% -> 0%
where the time goes in v1:
time: 473 us; the launch traced here: 463 us
  blocking collectives  300 us (63%)
  waiting for transfers between devices  90.4 us (19%)
  Pallas kernels  55.2 us (12%)
  starting transfers between devices  13.2 us (3%)
    all_to_all x21, blocking collectives, across(): v = lax.all_to_all(v, CHIPS, split_axis=0, concat_axis=0, tiled=True)  300 us
    ppermute x11, waiting for transfers between devices, relay(): lax.ppermute(v, 'section', [(i, (i + by) % sections) for i in range(secti...  69.6 us
    pallas_call x7, Pallas kernels, body(): kernel('experts', functools.partial(expert_kernel, when), (wide, *held),...  27.3 us
    pallas_call x3, Pallas kernels, body(): kernel('early_experts', functools.partial(early_expert_kernel, parts), (w...  11.4 us
  transfers between devices with their start and end apart: 15, of which 13 were waited for; matrix products, arithmetic and copies ran while one was open for 1% of the time, Pallas kernels for 0%

profile of v1, /device:TPU:8, one launch (start us, length us, event | category | flops | bytes accessed | tf_op | source)
XLA Modules:
  0.0 463.4 jit_solution(1893260153856380172)
XLA Ops:
  5.2 19.3 %all_to_all.110 = bf16[16,8,2048]{2,1,0:T(8,128)(2,1)S(1)} all-to-all(bf16[16,8,2048]{2,1,0:T(8,128)(2,1)S(1)} %bitcast.87), channel_id=1, replica_groups=mesh['section'=4,'x'=4,'z'=4,'core'=2] {'x','z'}, dimensions={0} | all-to-all | bytes 1048576 | tf_op jit(solution)/shard_map/all_to_all | solution.py:210
  28.5 7.7 %first_experts.1 = (bf16[128,2048]{1,0:T(8,128)(2,1)S(1)}, bf16[2,2,4096,384]{3,2,1,0:T(8,128)(2,1)S(1)}, bf16[2,2,4096,384]{3,2,1,0:T(8,128)(2,1)S(1)}, bf16[2,...) custom-call(bf16[128,2048]{1,0:T(8,128)(2,1)S(1)} %bitcast.64, bf16[2,1,2,4096,384]{4,3,2,1,0:T(8,128)(2,1)} %refs_0_.4, ...), custom_call_target="tpu_custom_call" | custom-call | tf_op jit(solution)/shard_map/first_experts/pallas_call | solution.py:225
  36.2 19.5 %all_to_all.111 = bf16[16,8,2048]{2,1,0:T(8,128)(2,1)S(1)} all-to-all(bf16[16,8,2048]{2,1,0:T(8,128)(2,1)S(1)} %bitcast.110), channel_id=1, replica_groups=mesh['section'=4,'x'=4,'z'=4,'core'=2] {'x','z'}, dimensions={0} | all-to-all | bytes 1048576 | tf_op jit(solution)/shard_map/all_to_all | solution.py:210
  63.1 13.9 %all_to_all.112 = bf16[16,8,2048]{2,1,0:T(8,128)(2,1)S(1)} all-to-all(bf16[16,8,2048]{2,1,0:T(8,128)(2,1)S(1)} %bitcast.88), channel_id=1, replica_groups=mesh['section'=4,'x'=4,'z'=4,'core'=2] {'x','z'}, dimensions={0} | all-to-all | bytes 1048576 | tf_op jit(solution)/shard_map/all_to_all | solution.py:210
  80.8 13.3 %all_to_all.113 = bf16[16,8,2048]{2,1,0:T(8,128)(2,1)S(1)} all-to-all(bf16[16,8,2048]{2,1,0:T(8,128)(2,1)S(1)} %bitcast.103), channel_id=1, replica_groups=mesh['section'=4,'x'=4,'z'=4,'core'=2] {'x','z'}, dimensions={0} | all-to-all | bytes 1048576 | tf_op jit(solution)/shard_map/all_to_all | solution.py:210
  101.3 13.6 %all_to_all.114 = bf16[16,8,2048]{2,1,0:T(8,128)(2,1)S(1)} all-to-all(bf16[16,8,2048]{2,1,0:T(8,128)(2,1)S(1)} %bitcast.89), channel_id=1, replica_groups=mesh['section'=4,'x'=4,'z'=4,'core'=2] {'x','z'}, dimensions={0} | all-to-all | bytes 1048576 | tf_op jit(solution)/shard_map/all_to_all | solution.py:210
  118.8 13.4 %all_to_all.115 = bf16[16,8,2048]{2,1,0:T(8,128)(2,1)S(1)} all-to-all(bf16[16,8,2048]{2,1,0:T(8,128)(2,1)S(1)} %bitcast.101), channel_id=1, replica_groups=mesh['section'=4,'x'=4,'z'=4,'core'=2] {'x','z'}, dimensions={0} | all-to-all | bytes 1048576 | tf_op jit(solution)/shard_map/all_to_all | solution.py:210
  134.1 5.7 %collective-permute-done.4.x = bf16[32,4096]{1,0:T(8,128)(2,1)S(1)} collective-permute-done((bf16[32,4096]{1,0:T(8,128)(2,1)S(1)}, bf16[32,4096]{1,0:T(8,128)(2,1)S(1)}, u32[]{:S(2)}, u32[]{:S(2)}) %collective-permute-start.4) | collective-permute-done | bytes 262176 | tf_op jit(solution)/shard_map/ppermute | solution.py:214
  140.2 13.3 %all_to_all.116 = bf16[16,8,2048]{2,1,0:T(8,128)(2,1)S(1)} all-to-all(bf16[16,8,2048]{2,1,0:T(8,128)(2,1)S(1)} %bitcast.90), channel_id=1, replica_groups=mesh['section'=4,'x'=4,'z'=4,'core'=2] {'x','z'}, dimensions={0} | all-to-all | bytes 1048576 | tf_op jit(solution)/shard_map/all_to_all | solution.py:210
  157.4 13.3 %all_to_all.117 = bf16[16,8,2048]{2,1,0:T(8,128)(2,1)S(1)} all-to-all(bf16[16,8,2048]{2,1,0:T(8,128)(2,1)S(1)} %bitcast.102), channel_id=1, replica_groups=mesh['section'=4,'x'=4,'z'=4,'core'=2] {'x','z'}, dimensions={0} | all-to-all | bytes 1048576 | tf_op jit(solution)/shard_map/all_to_all | solution.py:210
  171.8 6.9 %collective-permute-done.5.x = bf16[32,4096]{1,0:T(8,128)(2,1)S(1)} collective-permute-done((bf16[32,4096]{1,0:T(8,128)(2,1)S(1)}, bf16[32,4096]{1,0:T(8,128)(2,1)S(1)}, u32[]{:S(2)}, u32[]{:S(2)}) %collective-permute-start.5) | collective-permute-done | bytes 262176 | tf_op jit(solution)/shard_map/ppermute | solution.py:214
  179.1 15.2 %all_to_all.118 = bf16[16,8,2048]{2,1,0:T(8,128)(2,1)S(1)} all-to-all(bf16[16,8,2048]{2,1,0:T(8,128)(2,1)S(1)} %bitcast.91), channel_id=1, replica_groups=mesh['section'=4,'x'=4,'z'=4,'core'=2] {'x','z'}, dimensions={0} | all-to-all | bytes 1048576 | tf_op jit(solution)/shard_map/all_to_all | solution.py:210
  198.2 13.6 %all_to_all.119 = bf16[16,8,2048]{2,1,0:T(8,128)(2,1)S(1)} all-to-all(bf16[16,8,2048]{2,1,0:T(8,128)(2,1)S(1)} %bitcast.104), channel_id=1, replica_groups=mesh['section'=4,'x'=4,'z'=4,'core'=2] {'x','z'}, dimensions={0} | all-to-all | bytes 1048576 | tf_op jit(solution)/shard_map/all_to_all | solution.py:210
  212.2 7.6 %collective-permute-done.6.x = bf16[32,4096]{1,0:T(8,128)(2,1)S(1)} collective-permute-done((bf16[32,4096]{1,0:T(8,128)(2,1)S(1)}, bf16[32,4096]{1,0:T(8,128)(2,1)S(1)}, u32[]{:S(2)}, u32[]{:S(2)}) %collective-permute-start.6) | collective-permute-done | bytes 262176 | tf_op jit(solution)/shard_map/ppermute | solution.py:214
  220.2 13.6 %all_to_all.120 = bf16[16,8,2048]{2,1,0:T(8,128)(2,1)S(1)} all-to-all(bf16[16,8,2048]{2,1,0:T(8,128)(2,1)S(1)} %bitcast.92), channel_id=1, replica_groups=mesh['section'=4,'x'=4,'z'=4,'core'=2] {'x','z'}, dimensions={0} | all-to-all | bytes 1048576 | tf_op jit(solution)/shard_map/all_to_all | solution.py:210
  237.6 15.8 %all_to_all.121 = bf16[16,8,2048]{2,1,0:T(8,128)(2,1)S(1)} all-to-all(bf16[16,8,2048]{2,1,0:T(8,128)(2,1)S(1)} %bitcast.105), channel_id=1, replica_groups=mesh['section'=4,'x'=4,'z'=4,'core'=2] {'x','z'}, dimensions={0} | all-to-all | bytes 1048576 | tf_op jit(solution)/shard_map/all_to_all | solution.py:210
  253.8 7.3 %collective-permute-done.7.x = bf16[32,4096]{1,0:T(8,128)(2,1)S(1)} collective-permute-done((bf16[32,4096]{1,0:T(8,128)(2,1)S(1)}, bf16[32,4096]{1,0:T(8,128)(2,1)S(1)}, u32[]{:S(2)}, u32[]{:S(2)}) %collective-permute-start.7) | collective-permute-done | bytes 262176 | tf_op jit(solution)/shard_map/ppermute | solution.py:214
  261.6 13.6 %all_to_all.122 = bf16[16,8,2048]{2,1,0:T(8,128)(2,1)S(1)} all-to-all(bf16[16,8,2048]{2,1,0:T(8,128)(2,1)S(1)} %bitcast.93), channel_id=1, replica_groups=mesh['section'=4,'x'=4,'z'=4,'core'=2] {'x','z'}, dimensions={0} | all-to-all | bytes 1048576 | tf_op jit(solution)/shard_map/all_to_all | solution.py:210
  278.9 13.4 %all_to_all.123 = bf16[16,8,2048]{2,1,0:T(8,128)(2,1)S(1)} all-to-all(bf16[16,8,2048]{2,1,0:T(8,128)(2,1)S(1)} %bitcast.106), channel_id=1, replica_groups=mesh['section'=4,'x'=4,'z'=4,'core'=2] {'x','z'}, dimensions={0} | all-to-all | bytes 1048576 | tf_op jit(solution)/shard_map/all_to_all | solution.py:210
  292.7 7.6 %collective-permute-done.8.x = bf16[32,4096]{1,0:T(8,128)(2,1)S(1)} collective-permute-done((bf16[32,4096]{1,0:T(8,128)(2,1)S(1)}, bf16[32,4096]{1,0:T(8,128)(2,1)S(1)}, u32[]{:S(2)}, u32[]{:S(2)}) %collective-permute-start.8) | collective-permute-done | bytes 262176 | tf_op jit(solution)/shard_map/ppermute | solution.py:214
  300.7 13.3 %all_to_all.124 = bf16[16,8,2048]{2,1,0:T(8,128)(2,1)S(1)} all-to-all(bf16[16,8,2048]{2,1,0:T(8,128)(2,1)S(1)} %bitcast.94), channel_id=1, replica_groups=mesh['section'=4,'x'=4,'z'=4,'core'=2] {'x','z'}, dimensions={0} | all-to-all | bytes 1048576 | tf_op jit(solution)/shard_map/all_to_all | solution.py:210
  317.8 13.4 %all_to_all.125 = bf16[16,8,2048]{2,1,0:T(8,128)(2,1)S(1)} all-to-all(bf16[16,8,2048]{2,1,0:T(8,128)(2,1)S(1)} %bitcast.107), channel_id=1, replica_groups=mesh['section'=4,'x'=4,'z'=4,'core'=2] {'x','z'}, dimensions={0} | all-to-all | bytes 1048576 | tf_op jit(solution)/shard_map/all_to_all | solution.py:210
  331.6 7.6 %collective-permute-done.9.x = bf16[32,4096]{1,0:T(8,128)(2,1)S(1)} collective-permute-done((bf16[32,4096]{1,0:T(8,128)(2,1)S(1)}, bf16[32,4096]{1,0:T(8,128)(2,1)S(1)}, u32[]{:S(2)}, u32[]{:S(2)}) %collective-permute-start.9) | collective-permute-done | bytes 262176 | tf_op jit(solution)/shard_map/ppermute | solution.py:214
  339.6 13.5 %all_to_all.126 = bf16[16,8,2048]{2,1,0:T(8,128)(2,1)S(1)} all-to-all(bf16[16,8,2048]{2,1,0:T(8,128)(2,1)S(1)} %bitcast.95), channel_id=1, replica_groups=mesh['section'=4,'x'=4,'z'=4,'core'=2] {'x','z'}, dimensions={0} | all-to-all | bytes 1048576 | tf_op jit(solution)/shard_map/all_to_all | solution.py:210
  356.9 13.5 %all_to_all.127 = bf16[16,8,2048]{2,1,0:T(8,128)(2,1)S(1)} all-to-all(bf16[16,8,2048]{2,1,0:T(8,128)(2,1)S(1)} %bitcast.108), channel_id=1, replica_groups=mesh['section'=4,'x'=4,'z'=4,'core'=2] {'x','z'}, dimensions={0} | all-to-all | bytes 1048576 | tf_op jit(solution)/shard_map/all_to_all | solution.py:210
  370.8 7.5 %collective-permute-done.10.x = bf16[32,4096]{1,0:T(8,128)(2,1)S(1)} collective-permute-done((bf16[32,4096]{1,0:T(8,128)(2,1)S(1)}, bf16[32,4096]{1,0:T(8,128)(2,1)S(1)}, u32[]{:S(2)}, u32[]{:S(2)}) %collective-permute-start.10) | collective-permute-done | bytes 262176 | tf_op jit(solution)/shard_map/ppermute | solution.py:214
  378.7 13.3 %all_to_all.128 = bf16[16,8,2048]{2,1,0:T(8,128)(2,1)S(1)} all-to-all(bf16[16,8,2048]{2,1,0:T(8,128)(2,1)S(1)} %bitcast.96), channel_id=1, replica_groups=mesh['section'=4,'x'=4,'z'=4,'core'=2] {'x','z'}, dimensions={0} | all-to-all | bytes 1048576 | tf_op jit(solution)/shard_map/all_to_all | solution.py:210
  395.8 14.0 %all_to_all.129 = bf16[16,8,2048]{2,1,0:T(8,128)(2,1)S(1)} all-to-all(bf16[16,8,2048]{2,1,0:T(8,128)(2,1)S(1)} %bitcast.109), channel_id=1, replica_groups=mesh['section'=4,'x'=4,'z'=4,'core'=2] {'x','z'}, dimensions={0} | all-to-all | bytes 1048576 | tf_op jit(solution)/shard_map/all_to_all | solution.py:210
  410.2 9.6 %collective-permute-done.11.x = bf16[32,4096]{1,0:T(8,128)(2,1)S(1)} collective-permute-done((bf16[32,4096]{1,0:T(8,128)(2,1)S(1)}, bf16[32,4096]{1,0:T(8,128)(2,1)S(1)}, u32[]{:S(2)}, u32[]{:S(2)}) %collective-permute-start.11) | collective-permute-done | bytes 262176 | tf_op jit(solution)/shard_map/ppermute | solution.py:214
  420.2 13.9 %all_to_all.130 = bf16[16,8,2048]{2,1,0:T(8,128)(2,1)S(1)} all-to-all(bf16[16,8,2048]{2,1,0:T(8,128)(2,1)S(1)} %bitcast.86), channel_id=1, replica_groups=mesh['section'=4,'x'=4,'z'=4,'core'=2] {'x','z'}, dimensions={0} | all-to-all | bytes 1048576 | tf_op jit(solution)/shard_map/all_to_all | solution.py:210
  444.0 8.4 %all-to-all-done.21 = bf16[16,8,2048]{2,1,0:T(8,128)(2,1)S(1)} async-done(((bf16[16,8,2048]{2,1,0:T(8,128)(2,1)}), bf16[16,8,2048]{2,1,0:T(8,128)(2,1)S(1)}, u32[]{:S(2)}, u32[]{:S(2)}) %all-to-all-start.21) | async-done | bytes 524320 | tf_op jit(solution)/shard_map/all_to_all | solution.py:210
  454.0 8.5 %collective-permute-done.12 = bf16[32,4096]{1,0:T(8,128)(2,1)S(1)} collective-permute-done((bf16[32,4096]{1,0:T(8,128)(2,1)S(1)}, bf16[32,4096]{1,0:T(8,128)(2,1)S(1)}, u32[]{:S(2)}, u32[]{:S(2)}) %collective-permute-start.12) | collective-permute-done | bytes 262176 | tf_op jit(solution)/shard_map/ppermute | solution.py:258
  (59 shorter events, 78.6 us)
Async XLA Ops:
  0.0 28.5 %collective-permute-start = (bf16[2,1,2,4096,384]{4,3,2,1,0:T(8,128)(2,1)}, bf16[2,1,2,4096,384]{4,3,2,1,0:T(8,128)(2,1)}, u32[]{:S(2)}, u32[]{:S(2)}) collective-permute-start(bf16[2,1,2,4096,384]{4,3,2,1,0:T(8,128)(2,1)} %refs_0_.4), channel_id=1, source_target_pairs={{0,1},{1,0},{2,3},{3,2},{4,5},{5,4},{6,7},{7,6},{8,9},{9,8},{10,11... | collective-permute-start | bytes 37748744 | tf_op jit(solution)/shard_map/ppermute | solution.py:204
  0.0 28.5 %collective-permute-start.1 = (bf16[2,1,384,4096]{3,2,1,0:T(8,128)(2,1)}, bf16[2,1,384,4096]{3,2,1,0:T(8,128)(2,1)}, u32[]{:S(2)}, u32[]{:S(2)}) collective-permute-start(bf16[2,1,384,4096]{3,2,1,0:T(8,128)(2,1)} %refs_0_.5), channel_id=1, source_target_pairs={{0,1},{1,0},{2,3},{3,2},{4,5},{5,4},{6,7},{7,6},{8,9},{9,8},{10,11... | collective-permute-start | bytes 18874376 | tf_op jit(solution)/shard_map/ppermute | solution.py:204
  3.8 1.0 copy-start
  56.0 6.7 %collective-permute-start.2 = (bf16[32,4096]{1,0:T(8,128)(2,1)S(1)}, bf16[32,4096]{1,0:T(8,128)(2,1)S(1)}, u32[]{:S(2)}, u32[]{:S(2)}) collective-permute-start(bf16[32,4096]{1,0:T(8,128)(2,1)S(1)} %mix.11), channel_id=1, source_target_pairs={{0,32},{32,64},{64,96},{96,0},{1,33},{33,65},{65,97},{97,1},{2,34}... | collective-permute-start | bytes 786440 | tf_op jit(solution)/shard_map/ppermute | solution.py:214
  94.5 6.4 %collective-permute-start.3 = (bf16[32,4096]{1,0:T(8,128)(2,1)S(1)}, bf16[32,4096]{1,0:T(8,128)(2,1)S(1)}, u32[]{:S(2)}, u32[]{:S(2)}) collective-permute-start(bf16[32,4096]{1,0:T(8,128)(2,1)S(1)} %mix.12), channel_id=1, source_target_pairs={{0,32},{32,64},{64,96},{96,0},{1,33},{33,65},{65,97},{97,1},{2,34}... | collective-permute-start | bytes 786440 | tf_op jit(solution)/shard_map/ppermute | solution.py:214
  132.4 7.4 %collective-permute-start.4 = (bf16[32,4096]{1,0:T(8,128)(2,1)S(1)}, bf16[32,4096]{1,0:T(8,128)(2,1)S(1)}, u32[]{:S(2)}, u32[]{:S(2)}) collective-permute-start(bf16[32,4096]{1,0:T(8,128)(2,1)S(1)} %mix.13), channel_id=1, source_target_pairs={{0,32},{32,64},{64,96},{96,0},{1,33},{33,65},{65,97},{97,1},{2,34}... | collective-permute-start | bytes 786440 | tf_op jit(solution)/shard_map/ppermute | solution.py:214
  171.1 7.6 %collective-permute-start.5 = (bf16[32,4096]{1,0:T(8,128)(2,1)S(1)}, bf16[32,4096]{1,0:T(8,128)(2,1)S(1)}, u32[]{:S(2)}, u32[]{:S(2)}) collective-permute-start(bf16[32,4096]{1,0:T(8,128)(2,1)S(1)} %mix.14), channel_id=1, source_target_pairs={{0,32},{32,64},{64,96},{96,0},{1,33},{33,65},{65,97},{97,1},{2,34}... | collective-permute-start | bytes 786440 | tf_op jit(solution)/shard_map/ppermute | solution.py:214
  212.1 7.7 %collective-permute-start.6 = (bf16[32,4096]{1,0:T(8,128)(2,1)S(1)}, bf16[32,4096]{1,0:T(8,128)(2,1)S(1)}, u32[]{:S(2)}, u32[]{:S(2)}) collective-permute-start(bf16[32,4096]{1,0:T(8,128)(2,1)S(1)} %mix.15), channel_id=1, source_target_pairs={{0,32},{32,64},{64,96},{96,0},{1,33},{33,65},{65,97},{97,1},{2,34}... | collective-permute-start | bytes 786440 | tf_op jit(solution)/shard_map/ppermute | solution.py:214
  253.7 7.4 %collective-permute-start.7 = (bf16[32,4096]{1,0:T(8,128)(2,1)S(1)}, bf16[32,4096]{1,0:T(8,128)(2,1)S(1)}, u32[]{:S(2)}, u32[]{:S(2)}) collective-permute-start(bf16[32,4096]{1,0:T(8,128)(2,1)S(1)} %mix.16), channel_id=1, source_target_pairs={{0,32},{32,64},{64,96},{96,0},{1,33},{33,65},{65,97},{97,1},{2,34}... | collective-permute-start | bytes 786440 | tf_op jit(solution)/shard_map/ppermute | solution.py:214
  292.6 7.6 %collective-permute-start.8 = (bf16[32,4096]{1,0:T(8,128)(2,1)S(1)}, bf16[32,4096]{1,0:T(8,128)(2,1)S(1)}, u32[]{:S(2)}, u32[]{:S(2)}) collective-permute-start(bf16[32,4096]{1,0:T(8,128)(2,1)S(1)} %mix.17), channel_id=1, source_target_pairs={{0,32},{32,64},{64,96},{96,0},{1,33},{33,65},{65,97},{97,1},{2,34}... | collective-permute-start | bytes 786440 | tf_op jit(solution)/shard_map/ppermute | solution.py:214
  331.5 7.6 %collective-permute-start.9 = (bf16[32,4096]{1,0:T(8,128)(2,1)S(1)}, bf16[32,4096]{1,0:T(8,128)(2,1)S(1)}, u32[]{:S(2)}, u32[]{:S(2)}) collective-permute-start(bf16[32,4096]{1,0:T(8,128)(2,1)S(1)} %mix.18), channel_id=1, source_target_pairs={{0,32},{32,64},{64,96},{96,0},{1,33},{33,65},{65,97},{97,1},{2,34}... | collective-permute-start | bytes 786440 | tf_op jit(solution)/shard_map/ppermute | solution.py:214
  370.7 7.6 %collective-permute-start.10 = (bf16[32,4096]{1,0:T(8,128)(2,1)S(1)}, bf16[32,4096]{1,0:T(8,128)(2,1)S(1)}, u32[]{:S(2)}, u32[]{:S(2)}) collective-permute-start(bf16[32,4096]{1,0:T(8,128)(2,1)S(1)} %mix.19), channel_id=1, source_target_pairs={{0,32},{32,64},{64,96},{96,0},{1,33},{33,65},{65,97},{97,1},{2,34}... | collective-permute-start | bytes 786440 | tf_op jit(solution)/shard_map/ppermute | solution.py:214
  410.1 9.7 %collective-permute-start.11 = (bf16[32,4096]{1,0:T(8,128)(2,1)S(1)}, bf16[32,4096]{1,0:T(8,128)(2,1)S(1)}, u32[]{:S(2)}, u32[]{:S(2)}) collective-permute-start(bf16[32,4096]{1,0:T(8,128)(2,1)S(1)} %mix.20), channel_id=1, source_target_pairs={{0,32},{32,64},{64,96},{96,0},{1,33},{33,65},{65,97},{97,1},{2,34}... | collective-permute-start | bytes 786440 | tf_op jit(solution)/shard_map/ppermute | solution.py:214
  438.7 13.6 %all-to-all-start.21 = ((bf16[16,8,2048]{2,1,0:T(8,128)(2,1)}), bf16[16,8,2048]{2,1,0:T(8,128)(2,1)S(1)}, u32[]{:S(2)}, u32[]{:S(2)}) async-start(bf16[16,8,2048]{2,1,0:T(8,128)(2,1)} %bitcast.46), calls=%async_computation.21 | async-start | bytes 1048576 | tf_op jit(solution)/shard_map/all_to_all | solution.py:210
  442.3 11.7 %collective-permute-start.13 = (bf16[32,4096]{1,0:T(8,128)(2,1)S(1)}, bf16[32,4096]{1,0:T(8,128)(2,1)S(1)}, u32[]{:S(2)}, u32[]{:S(2)}) collective-permute-start(bf16[32,4096]{1,0:T(8,128)(2,1)S(1)} %collective-permute-done.11.x), channel_id=1, source_target_pairs={{0,64},{32,96},{64,0},{96,32},{1,65},{33,97},{65,1},{97,33},{2,66}... | collective-permute-start | bytes 786440 | tf_op jit(solution)/shard_map/ppermute | solution.py:214
  452.7 9.8 %collective-permute-start.12 = (bf16[32,4096]{1,0:T(8,128)(2,1)S(1)}, bf16[32,4096]{1,0:T(8,128)(2,1)S(1)}, u32[]{:S(2)}, u32[]{:S(2)}) collective-permute-start(bf16[32,4096]{1,0:T(8,128)(2,1)S(1)} %mix.21), channel_id=1, source_target_pairs={{96,32},{97,33},{98,34},{99,35},{100,36},{101,37},{102,38},{103,39... | collective-permute-start | bytes 786440 | tf_op jit(solution)/shard_map/ppermute | solution.py:258

commit v2 on v1

v2 whole, which is shorter than its diff:
```python
import functools

import jax
import jax.numpy as jnp
from jax import lax
from jax.experimental import pallas as pl
from jax.experimental.pallas import tpu as pltpu
from jax.sharding import Mesh
from jax.sharding import PartitionSpec as P

SPLIT = 4
CAP = 4
CHIPS = ("x", "z")
SWAP = [(0, 1), (1, 0)]

IN_VMEM = pl.BlockSpec(memory_space=pltpu.VMEM)
IN_SMEM = pl.BlockSpec(memory_space=pltpu.SMEM)
IN_HBM = pl.BlockSpec(memory_space=pltpu.HBM)
MIB = 2**20


def dot(a, b):
    return jnp.dot(a, b, preferred_element_type=jnp.float32)


def dot_first(a, b):
    return lax.dot_general(a, b, (((0,), (0,)), ((), ())), preferred_element_type=jnp.float32)


def as_bf16(mask):
    return mask.astype(jnp.float32).astype(jnp.bfloat16)


def schedule(step, section, sections, layers):
    behind = step - section[0]
    micro = lax.rem(behind + sections, sections)
    repeat = jnp.where(behind >= sections, 1, 0)
    active = jnp.logical_and(behind >= 0, behind < layers)
    return repeat, repeat * sections + micro, active


def relay_pairs(step, sections, layers):
    if step == 0:
        return [(k, k ^ 1) for k in range(sections)]
    home = step - layers + 1
    if home < 1:
        return [(k, (k + 1) % sections) for k in range(sections)]
    return [(k, k) for k in range(home)] + [(k, k + 1) for k in range(home, sections - 1)] + [(sections - 1, home)]


def make_tables(ids, gates, hot, mix):
    repeats, _, micros, topk, rows = ids.shape
    wide = hot.shape[1]
    place = lax.broadcasted_iota(jnp.int32, (wide, rows), 0)
    expert = place // (2 * CAP * (SPLIT // 2))
    slot = place - place // CAP * CAP
    half = place // CAP - place // (2 * CAP) * 2
    earlier = as_bf16(lax.broadcasted_iota(jnp.int32, (rows, rows), 0) < lax.broadcasted_iota(jnp.int32, (rows, rows), 1))
    for group in range(repeats * micros):
        named = ids[group // micros, 0, group % micros]
        given = gates[group // micros, 0, group % micros]
        chosen = jnp.zeros((wide, rows), jnp.float32)
        weight = jnp.zeros((wide, rows), jnp.float32)
        for k in range(topk):
            match = named[k : k + 1, :] == expert
            chosen = jnp.where(match, 1.0, chosen)
            weight = jnp.where(match, weight + given[k : k + 1, :], weight)
        position = dot(chosen.astype(jnp.bfloat16), earlier)
        taken = jnp.where(position == slot.astype(jnp.float32), chosen, 0.0)
        here = jnp.concatenate([jnp.where(half == k, taken, 0.0) for k in range(2)], axis=1)
        scaled = here * jnp.concatenate([weight, weight], axis=1)
        high = scaled.astype(jnp.bfloat16)
        hot[group] = here.astype(jnp.bfloat16)
        mix[0, group] = high
        mix[1, group] = (scaled - high.astype(jnp.float32)).astype(jnp.bfloat16)


def pack_kernel(when, section, x, gain, hot, out):
    repeat, group, _ = when(section)
    values = x[...].astype(jnp.float32)
    scale = lax.rsqrt(jnp.mean(values * values, axis=-1, keepdims=True) + 1e-06)
    normed = (values * scale * gain[repeat]).astype(jnp.bfloat16)
    half = normed.shape[1] // 2
    stacked = jnp.concatenate([normed[:, :half], normed[:, half:]], axis=0)
    out[...] = dot(hot[group], stacked).astype(jnp.bfloat16)


def first_pack_kernel(when, section, x, gain, ids, gates, out, hot, mix):
    make_tables(ids, gates, hot, mix)
    pack_kernel(when, section, x, gain, hot, out)


def place(rows, columns, offset, transposed):
    shape = (columns, rows) if transposed else (rows, columns)
    row = lax.broadcasted_iota(jnp.int32, shape, int(transposed))
    column = lax.broadcasted_iota(jnp.int32, shape, 1 - int(transposed))
    block = column // (2 * CAP)
    inner = column - block * (2 * CAP) - offset
    return as_bf16((block * CAP + inner == row) & (inner >= 0) & (inner < CAP))


def gather_rows(rows, x, start=0):
    wide, half = rows.shape
    got = rows[...]
    for k in range(2):
        x[start : start + wide // 2, k * half : (k + 1) * half] = dot(place(wide // 2, wide, k * CAP, False), got).astype(jnp.bfloat16)


def gated(gate, upward):
    return (gate / (1.0 + jnp.exp(-gate)) * upward).astype(jnp.bfloat16)


def dot_halves(x, held, repeat, columns):
    half = x.shape[1] // 2
    return dot(x[:, :half], held[0][repeat, :, columns]) + dot(x[:, half:], held[1][repeat, :, columns])


def core_hidden(x, held, repeat, who):
    size = held[0].shape[2] // 4
    return gated(*(dot_halves(x, held, repeat, slice((2 * g + who) * size, (2 * g + who + 1) * size)) for g in range(2)))


def down_rows(hidden, downs, out):
    count = hidden.shape[0]
    spread = [dot(place(count, 2 * count, k * CAP, True), hidden).astype(jnp.bfloat16) for k in range(2)]
    pieces = 4
    size = out.shape[1] // pieces
    for j in range(pieces):
        columns = slice(j * size, (j + 1) * size)
        total = dot(spread[0], downs[0][:, columns]) + dot(spread[1], downs[1][:, columns])
        out[:, columns] = total.astype(out.dtype)


def weight_copies(w_in, w_down, repeat, who, held, sems):
    half = held[0].shape[1]
    size = w_in.shape[4]
    pairs = []
    for k in range(2):
        part = pl.ds(k * half, half)
        for g in range(2):
            pairs.append((w_in.at[repeat, 0, g, part, :], held[k].at[repeat, :, pl.ds((2 * g + who) * size, size)]))
    for k in range(2):
        part = pl.ds(k * half, half)
        pairs.append((w_down.at[repeat, 0, :, part], held[2 + k].at[repeat, pl.ds(who * size, size), :]))
    copies = [pltpu.make_async_copy(source, to, sems.at[n]) for n, (source, to) in enumerate(pairs)]
    for copy in copies:
        copy.start()
    return copies


def first_expert_kernel(rows, rows_other, w_in, w_down, out, out_other, *refs):
    held, (x, sems) = refs[:4], refs[4:]
    copies = weight_copies(w_in, w_down, 0, 0, held, sems)
    count = rows.shape[0] // 2
    gather_rows(rows, x)
    gather_rows(rows_other, x, count)
    for copy in copies[:4]:
        copy.wait()
    hidden = core_hidden(x, held, 0, 0)
    for copy in copies[4:]:
        copy.wait()
    size = hidden.shape[1]
    downs = [w.at[0, :size] for w in held[2:]]
    down_rows(hidden[count:], downs, out_other)
    down_rows(hidden[:count], downs, out)


def add_kernel(a, b, out):
    out[...] = (a[...] + b[...].astype(jnp.float32)).astype(jnp.bfloat16)


def experts(rows, x, held, repeat, out):
    gather_rows(rows, x)
    both = dot_halves(x, held, repeat, slice(None))
    size = both.shape[1] // 2
    down_rows(gated(both[:, :size], both[:, size:]), [w.at[repeat] for w in held[2:]], out)


def second_expert_kernel(rows, w_in, w_down, *refs):
    held, out, after, (x, sems) = refs[:4], refs[4], refs[5:9], refs[9:]
    copies = weight_copies(w_in, w_down, 0, 1, after, sems)
    gather_rows(rows, x)
    hidden = [core_hidden(x, held, 0, 0)]
    for copy in copies[:4]:
        copy.wait()
    hidden.append(core_hidden(x, after, 0, 1))
    for copy in copies[4:]:
        copy.wait()
    down_rows(jnp.concatenate(hidden, axis=1), [w.at[0] for w in after[2:]], out)


def early_expert_kernel(who, rows, w_in, w_down, *refs):
    held, out, after, (x, sems) = refs[:4], refs[4], refs[5:9], refs[9:]
    copies = weight_copies(w_in, w_down, 1, who, after, sems)
    experts(rows, x, held, 0, out)
    for copy in copies:
        copy.wait()


def expert_kernel(when, section, rows, *refs):
    repeat, _, _ = when(section)
    experts(rows, refs[-1], refs[:4], repeat, refs[4])


def mix_kernel(when, section, x, returned, mix, out):
    _, group, active = when(section)
    got = returned[...]
    update = dot_first(mix[0, group], got) + dot_first(mix[1, group], got)
    rows = x.shape[0]
    update = jnp.concatenate([update[:rows], update[rows:]], axis=1)
    values = x[...].astype(jnp.float32)
    out[...] = jnp.where(active, values + update, values).astype(jnp.bfloat16)


def kernel(name, function, out_shape, in_specs, limit=4, scratch=(), aliases=None):
    return pl.pallas_call(
        function,
        out_shape=out_shape,
        in_specs=in_specs,
        out_specs=jax.tree.map(lambda _: IN_VMEM, out_shape),
        scratch_shapes=list(scratch),
        input_output_aliases=aliases or {},
        compiler_params=pltpu.CompilerParams(vmem_limit_bytes=limit * MIB),
        name=name,
    )


def body(tokens, w_in, w_down, norm_gain, route_ids, gate_values):
    sections = lax.axis_size("section")
    chips = lax.axis_size("x") * lax.axis_size("z")
    repeats, _, micros, rows, _ = route_ids.shape
    layers = repeats * sections
    steps = layers + sections - 1
    groups = repeats * micros
    section = lax.axis_index("section").astype(jnp.int32).reshape(1)
    width = tokens.shape[-1]
    slots = chips * 2 * CAP
    bf16 = lambda *shape: jax.ShapeDtypeStruct(shape, jnp.bfloat16)

    def kept(*arrays):
        return [pltpu.with_memory_space_constraint(a, pltpu.VMEM) for a in arrays]

    def outside(*arrays):
        return [pltpu.with_memory_space_constraint(a, pltpu.HBM) for a in arrays]

    hidden = w_in.shape[-1]
    held = (pltpu.VMEM((repeats, width // 2, 4 * hidden), jnp.bfloat16),) * 2 + (
        pltpu.VMEM((repeats, 2 * hidden, width // 2), jnp.bfloat16),
    ) * 2
    wide = bf16(slots, width // 2)
    dma = pltpu.SemaphoreType.DMA((6,))

    def across(v):
        v = v.reshape(chips, 2 * CAP, width // 2)
        v = lax.all_to_all(v, CHIPS, split_axis=0, concat_axis=0, tiled=True)
        return v.reshape(slots, width // 2)

    def other_core(v):
        return lax.ppermute(v, "core", SWAP)

    state = tokens[0]
    for step in range(steps):
        when = functools.partial(schedule, step, sections=sections, layers=layers)
        if step == 0:
            packed, hot, mix = kernel(
                "first_norm_pack",
                functools.partial(first_pack_kernel, when),
                (wide, bf16(groups, slots, 2 * rows), bf16(2, groups, slots, 2 * rows)),
                [IN_SMEM] + [IN_VMEM] * 4,
            )(section, *outside(state, norm_gain, jnp.swapaxes(route_ids, 3, 4), jnp.swapaxes(gate_values, 3, 4)))
        else:
            packed = kernel("norm_pack", functools.partial(pack_kernel, when), wide, [IN_SMEM] + [IN_VMEM] * 3)(
                section, state, norm_gain, hot
            )
        arrived = across(packed)
        x = pltpu.VMEM((slots // 2, width), jnp.bfloat16)
        if step == 0:
            own, outputs, *weights = kernel(
                "first_experts",
                first_expert_kernel,
                (jax.ShapeDtypeStruct(wide.shape, jnp.float32), wide, *held),
                [IN_VMEM] * 2 + [IN_HBM] * 2,
                scratch=[pltpu.VMEM((slots, width), jnp.bfloat16), dma],
                limit=6,
            )(arrived, other_core(arrived), *outside(w_in, w_down))
            outputs = kernel("add", add_kernel, wide, [IN_VMEM] * 2)(own, other_core(outputs))
            late_in, late_down, outputs = lax.optimization_barrier((w_in, w_down, outputs))
            sources = ((w_in, w_down), (other_core(late_in), other_core(late_down)))
        elif step == 1:
            outputs, *weights = kernel(
                "second_experts",
                second_expert_kernel,
                (wide, *held),
                [IN_VMEM] + [IN_HBM] * 2 + [IN_VMEM] * 4,
                scratch=[x, dma],
                aliases={3 + k: 1 + k for k in range(4)},
            )(arrived, *outside(*sources[1]), *kept(*weights))
        elif step < 4:
            outputs, *weights = kernel(
                "early_experts",
                functools.partial(early_expert_kernel, step - 2),
                (wide, *held),
                [IN_VMEM] + [IN_HBM] * 2 + [IN_VMEM] * 4,
                scratch=[x, dma],
                aliases={3 + k: 1 + k for k in range(4)},
            )(arrived, *outside(*sources[step - 2]), *kept(*weights))
        else:
            outputs, *weights = kernel(
                "experts",
                functools.partial(expert_kernel, when),
                (wide, *held),
                [IN_SMEM] + [IN_VMEM] * 5,
                scratch=[x],
                aliases={2 + k: 1 + k for k in range(4)},
            )(section, arrived, *kept(*weights))
        returned = across(outputs)
        state = kernel("mix", functools.partial(mix_kernel, when), bf16(rows, width), [IN_SMEM] + [IN_VMEM] * 3)(
            section, state, returned, mix
        )
        if step < steps - 1:
            state = lax.ppermute(state, "section", relay_pairs(step, sections, layers))
    return state[None]


def solution(mesh):
    fine = Mesh(mesh.devices.reshape(4, 4, 4, 2), ("section", "x", "z", "core"))
    expert = ("x", "z", "core")
    return jax.shard_map(
        body,
        mesh=fine,
        in_specs=(
            P("section", expert, None),
            P(None, "section", None, None, expert),
            P(None, "section", expert, None),
            P(None, "section", None),
            P(None, "section", None, expert, None),
            P(None, "section", None, expert, None),
        ),
        out_specs=P("section", expert, None),
        check_vma=False,
    )
```

time: 473 us -> 452 us (0.956)
  the two profiles are of different devices: /device:TPU:8 before, /device:TPU:24 now
where the time goes in v2:
time: 452 us; the launch traced here: 443 us
  blocking collectives  309 us (68%)
  Pallas kernels  55.2 us (12%)
  waiting for transfers between devices  50.9 us (11%)
  starting transfers between devices  27.1 us (6%)
    all_to_all x22, blocking collectives, across(): v = lax.all_to_all(v, CHIPS, split_axis=0, concat_axis=0, tiled=True)  309 us
    ppermute x10, waiting for transfers between devices, body(): state = lax.ppermute(state, 'section', relay_pairs(step, sections, layers))  47.2 us
    ppermute x10, starting transfers between devices, body(): state = lax.ppermute(state, 'section', relay_pairs(step, sections, layers))  26.3 us
    pallas_call x7, Pallas kernels, body(): kernel('experts', functools.partial(expert_kernel, when), (wide, *held),...  25.5 us
  transfers between devices with their start and end apart: 14, of which 12 were waited for; matrix products, arithmetic and copies ran while one was open for 0% of the time, Pallas kernels for 0%

profile of v2, /device:TPU:24, one launch (start us, length us, event | category | flops | bytes accessed | tf_op | source)
XLA Modules:
  0.0 443.3 jit_solution(9145876057915255126)
XLA Ops:
  2.4 19.2 %all_to_all.110 = bf16[16,8,2048]{2,1,0:T(8,128)(2,1)S(1)} all-to-all(bf16[16,8,2048]{2,1,0:T(8,128)(2,1)S(1)} %bitcast.95), channel_id=1, replica_groups=mesh['section'=4,'x'=4,'z'=4,'core'=2] {'x','z'}, dimensions={0} | all-to-all | bytes 1048576 | tf_op jit(solution)/shard_map/all_to_all | solution.py:255
  23.4 5.8 %first_experts.1 = (f32[128,2048]{1,0:T(8,128)S(1)}, bf16[128,2048]{1,0:T(8,128)(2,1)S(1)}, bf16[2,2048,1536]{2,1,0:T(8,128)(2,1)S(1)}, bf16[2,2048,1536]{2,1,0:...) custom-call(bf16[128,2048]{1,0:T(8,128)(2,1)S(1)} %bitcast.60, ...), custom_call_target="tpu_custom_call" | custom-call | tf_op jit(solution)/shard_map/first_experts/pallas_call | solution.py:278
  31.9 15.1 %all_to_all.111 = bf16[16,8,2048]{2,1,0:T(8,128)(2,1)S(1)} all-to-all(bf16[16,8,2048]{2,1,0:T(8,128)(2,1)S(1)} %bitcast.82), channel_id=1, replica_groups=mesh['section'=4,'x'=4,'z'=4,'core'=2] {'x','z'}, dimensions={0} | all-to-all | bytes 1048576 | tf_op jit(solution)/shard_map/all_to_all | solution.py:255
  48.2 5.9 %collective-permute-done.2.x = bf16[32,4096]{1,0:T(8,128)(2,1)S(1)} collective-permute-done((bf16[32,4096]{1,0:T(8,128)(2,1)S(1)}, bf16[32,4096]{1,0:T(8,128)(2,1)S(1)}, u32[]{:S(2)}, u32[]{:S(2)}) %collective-permute-start.2) | collective-permute-done | bytes 262176 | tf_op jit(solution)/shard_map/ppermute | solution.py:321
  54.5 13.9 %all_to_all.112 = bf16[16,8,2048]{2,1,0:T(8,128)(2,1)S(1)} all-to-all(bf16[16,8,2048]{2,1,0:T(8,128)(2,1)S(1)} %bitcast.73), channel_id=1, replica_groups=mesh['section'=4,'x'=4,'z'=4,'core'=2] {'x','z'}, dimensions={0} | all-to-all | bytes 1048576 | tf_op jit(solution)/shard_map/all_to_all | solution.py:255
  68.4 5.2 %second_experts.1 = (bf16[128,2048]{1,0:T(8,128)(2,1)S(1)}, bf16[2,2048,1536]{2,1,0:T(8,128)(2,1)S(1)}, bf16[2,2048,1536]{2,1,0:T(8,128)(2,1)S(1)}, bf16[2,768,2...) custom-call(bf16[128,2048]{1,0:T(8,128)(2,1)S(1)} %bitcast.49, ...), custom_call_target="tpu_custom_call", output_to_operand_aliasing={{1}: (3, {}), {2}: (4, {}), {3}: (5, {}), {4}: (6, {})} | custom-call | tf_op jit(solution)/shard_map/second_experts/pallas_call | solution.py:290
  73.7 13.3 %all_to_all.113 = bf16[16,8,2048]{2,1,0:T(8,128)(2,1)S(1)} all-to-all(bf16[16,8,2048]{2,1,0:T(8,128)(2,1)S(1)} %bitcast.86), channel_id=1, replica_groups=mesh['section'=4,'x'=4,'z'=4,'core'=2] {'x','z'}, dimensions={0} | all-to-all | bytes 1048576 | tf_op jit(solution)/shard_map/all_to_all | solution.py:255
  87.7 6.1 %collective-permute-done.5.x = bf16[32,4096]{1,0:T(8,128)(2,1)S(1)} collective-permute-done((bf16[32,4096]{1,0:T(8,128)(2,1)S(1)}, bf16[32,4096]{1,0:T(8,128)(2,1)S(1)}, u32[]{:S(2)}, u32[]{:S(2)}) %collective-permute-start.5) | collective-permute-done | bytes 262176 | tf_op jit(solution)/shard_map/ppermute | solution.py:321
  94.2 13.5 %all_to_all.114 = bf16[16,8,2048]{2,1,0:T(8,128)(2,1)S(1)} all-to-all(bf16[16,8,2048]{2,1,0:T(8,128)(2,1)S(1)} %bitcast.74), channel_id=1, replica_groups=mesh['section'=4,'x'=4,'z'=4,'core'=2] {'x','z'}, dimensions={0} | all-to-all | bytes 1048576 | tf_op jit(solution)/shard_map/all_to_all | solution.py:255
  111.5 13.4 %all_to_all.115 = bf16[16,8,2048]{2,1,0:T(8,128)(2,1)S(1)} all-to-all(bf16[16,8,2048]{2,1,0:T(8,128)(2,1)S(1)} %bitcast.87), channel_id=1, replica_groups=mesh['section'=4,'x'=4,'z'=4,'core'=2] {'x','z'}, dimensions={0} | all-to-all | bytes 1048576 | tf_op jit(solution)/shard_map/all_to_all | solution.py:255
  126.8 4.9 %collective-permute-done.6.x = bf16[32,4096]{1,0:T(8,128)(2,1)S(1)} collective-permute-done((bf16[32,4096]{1,0:T(8,128)(2,1)S(1)}, bf16[32,4096]{1,0:T(8,128)(2,1)S(1)}, u32[]{:S(2)}, u32[]{:S(2)}) %collective-permute-start.6) | collective-permute-done | bytes 262176 | tf_op jit(solution)/shard_map/ppermute | solution.py:321
  132.1 13.5 %all_to_all.116 = bf16[16,8,2048]{2,1,0:T(8,128)(2,1)S(1)} all-to-all(bf16[16,8,2048]{2,1,0:T(8,128)(2,1)S(1)} %bitcast.75), channel_id=1, replica_groups=mesh['section'=4,'x'=4,'z'=4,'core'=2] {'x','z'}, dimensions={0} | all-to-all | bytes 1048576 | tf_op jit(solution)/shard_map/all_to_all | solution.py:255
  149.4 13.2 %all_to_all.117 = bf16[16,8,2048]{2,1,0:T(8,128)(2,1)S(1)} all-to-all(bf16[16,8,2048]{2,1,0:T(8,128)(2,1)S(1)} %bitcast.85), channel_id=1, replica_groups=mesh['section'=4,'x'=4,'z'=4,'core'=2] {'x','z'}, dimensions={0} | all-to-all | bytes 1048576 | tf_op jit(solution)/shard_map/all_to_all | solution.py:255
  165.7 3.9 collective-permute-done.7.x
  170.0 14.7 %all_to_all.118 = bf16[16,8,2048]{2,1,0:T(8,128)(2,1)S(1)} all-to-all(bf16[16,8,2048]{2,1,0:T(8,128)(2,1)S(1)} %bitcast.76), channel_id=1, replica_groups=mesh['section'=4,'x'=4,'z'=4,'core'=2] {'x','z'}, dimensions={0} | all-to-all | bytes 1048576 | tf_op jit(solution)/shard_map/all_to_all | solution.py:255
  188.4 13.6 %all_to_all.119 = bf16[16,8,2048]{2,1,0:T(8,128)(2,1)S(1)} all-to-all(bf16[16,8,2048]{2,1,0:T(8,128)(2,1)S(1)} %bitcast.88), channel_id=1, replica_groups=mesh['section'=4,'x'=4,'z'=4,'core'=2] {'x','z'}, dimensions={0} | all-to-all | bytes 1048576 | tf_op jit(solution)/shard_map/all_to_all | solution.py:255
  202.3 4.0 collective-permute-start.8
  210.6 13.6 %all_to_all.120 = bf16[16,8,2048]{2,1,0:T(8,128)(2,1)S(1)} all-to-all(bf16[16,8,2048]{2,1,0:T(8,128)(2,1)S(1)} %bitcast.77), channel_id=1, replica_groups=mesh['section'=4,'x'=4,'z'=4,'core'=2] {'x','z'}, dimensions={0} | all-to-all | bytes 1048576 | tf_op jit(solution)/shard_map/all_to_all | solution.py:255
  227.9 15.9 %all_to_all.121 = bf16[16,8,2048]{2,1,0:T(8,128)(2,1)S(1)} all-to-all(bf16[16,8,2048]{2,1,0:T(8,128)(2,1)S(1)} %bitcast.89), channel_id=1, replica_groups=mesh['section'=4,'x'=4,'z'=4,'core'=2] {'x','z'}, dimensions={0} | all-to-all | bytes 1048576 | tf_op jit(solution)/shard_map/all_to_all | solution.py:255
  251.9 13.4 %all_to_all.122 = bf16[16,8,2048]{2,1,0:T(8,128)(2,1)S(1)} all-to-all(bf16[16,8,2048]{2,1,0:T(8,128)(2,1)S(1)} %bitcast.78), channel_id=1, replica_groups=mesh['section'=4,'x'=4,'z'=4,'core'=2] {'x','z'}, dimensions={0} | all-to-all | bytes 1048576 | tf_op jit(solution)/shard_map/all_to_all | solution.py:255
  269.0 13.3 %all_to_all.123 = bf16[16,8,2048]{2,1,0:T(8,128)(2,1)S(1)} all-to-all(bf16[16,8,2048]{2,1,0:T(8,128)(2,1)S(1)} %bitcast.90), channel_id=1, replica_groups=mesh['section'=4,'x'=4,'z'=4,'core'=2] {'x','z'}, dimensions={0} | all-to-all | bytes 1048576 | tf_op jit(solution)/shard_map/all_to_all | solution.py:255
  290.8 13.3 %all_to_all.124 = bf16[16,8,2048]{2,1,0:T(8,128)(2,1)S(1)} all-to-all(bf16[16,8,2048]{2,1,0:T(8,128)(2,1)S(1)} %bitcast.79), channel_id=1, replica_groups=mesh['section'=4,'x'=4,'z'=4,'core'=2] {'x','z'}, dimensions={0} | all-to-all | bytes 1048576 | tf_op jit(solution)/shard_map/all_to_all | solution.py:255
  307.8 13.3 %all_to_all.125 = bf16[16,8,2048]{2,1,0:T(8,128)(2,1)S(1)} all-to-all(bf16[16,8,2048]{2,1,0:T(8,128)(2,1)S(1)} %bitcast.91), channel_id=1, replica_groups=mesh['section'=4,'x'=4,'z'=4,'core'=2] {'x','z'}, dimensions={0} | all-to-all | bytes 1048576 | tf_op jit(solution)/shard_map/all_to_all | solution.py:255
  321.5 4.0 collective-permute-start.11
  329.8 13.3 %all_to_all.126 = bf16[16,8,2048]{2,1,0:T(8,128)(2,1)S(1)} all-to-all(bf16[16,8,2048]{2,1,0:T(8,128)(2,1)S(1)} %bitcast.80), channel_id=1, replica_groups=mesh['section'=4,'x'=4,'z'=4,'core'=2] {'x','z'}, dimensions={0} | all-to-all | bytes 1048576 | tf_op jit(solution)/shard_map/all_to_all | solution.py:255
  346.8 13.4 %all_to_all.127 = bf16[16,8,2048]{2,1,0:T(8,128)(2,1)S(1)} all-to-all(bf16[16,8,2048]{2,1,0:T(8,128)(2,1)S(1)} %bitcast.92), channel_id=1, replica_groups=mesh['section'=4,'x'=4,'z'=4,'core'=2] {'x','z'}, dimensions={0} | all-to-all | bytes 1048576 | tf_op jit(solution)/shard_map/all_to_all | solution.py:255
  364.4 4.4 %collective-permute-done.12.x = bf16[32,4096]{1,0:T(8,128)(2,1)S(1)} collective-permute-done((bf16[32,4096]{1,0:T(8,128)(2,1)S(1)}, bf16[32,4096]{1,0:T(8,128)(2,1)S(1)}, u32[]{:S(2)}, u32[]{:S(2)}) %collective-permute-start.12) | collective-permute-done | bytes 262176 | tf_op jit(solution)/shard_map/ppermute | solution.py:321
  369.2 13.5 %all_to_all.128 = bf16[16,8,2048]{2,1,0:T(8,128)(2,1)S(1)} all-to-all(bf16[16,8,2048]{2,1,0:T(8,128)(2,1)S(1)} %bitcast.81), channel_id=1, replica_groups=mesh['section'=4,'x'=4,'z'=4,'core'=2] {'x','z'}, dimensions={0} | all-to-all | bytes 1048576 | tf_op jit(solution)/shard_map/all_to_all | solution.py:255
  386.4 14.9 %all_to_all.129 = bf16[16,8,2048]{2,1,0:T(8,128)(2,1)S(1)} all-to-all(bf16[16,8,2048]{2,1,0:T(8,128)(2,1)S(1)} %bitcast.93), channel_id=1, replica_groups=mesh['section'=4,'x'=4,'z'=4,'core'=2] {'x','z'}, dimensions={0} | all-to-all | bytes 1048576 | tf_op jit(solution)/shard_map/all_to_all | solution.py:255
  403.6 6.3 %collective-permute-done.13.x = bf16[32,4096]{1,0:T(8,128)(2,1)S(1)} collective-permute-done((bf16[32,4096]{1,0:T(8,128)(2,1)S(1)}, bf16[32,4096]{1,0:T(8,128)(2,1)S(1)}, u32[]{:S(2)}, u32[]{:S(2)}) %collective-permute-start.13) | collective-permute-done | bytes 262176 | tf_op jit(solution)/shard_map/ppermute | solution.py:321
  410.4 14.4 %all_to_all.130 = bf16[16,8,2048]{2,1,0:T(8,128)(2,1)S(1)} all-to-all(bf16[16,8,2048]{2,1,0:T(8,128)(2,1)S(1)} %bitcast.72), channel_id=1, replica_groups=mesh['section'=4,'x'=4,'z'=4,'core'=2] {'x','z'}, dimensions={0} | all-to-all | bytes 1048576 | tf_op jit(solution)/shard_map/all_to_all | solution.py:255
  428.5 13.3 %all_to_all.131 = bf16[16,8,2048]{2,1,0:T(8,128)(2,1)S(1)} all-to-all(bf16[16,8,2048]{2,1,0:T(8,128)(2,1)S(1)} %bitcast.94), channel_id=1, replica_groups=mesh['section'=4,'x'=4,'z'=4,'core'=2] {'x','z'}, dimensions={0} | all-to-all | bytes 1048576 | tf_op jit(solution)/shard_map/all_to_all | solution.py:255
  (61 shorter events, 82.6 us)
Async XLA Ops:
  0.0 47.0 %copy-start.1 = (bf16[1,32,4096]{2,1,0:T(8,128)(2,1)S(1)}, bf16[1,32,4096]{2,1,0:T(8,128)(2,1)}, u32[]{:S(2)}) copy-start(bf16[1,32,4096]{2,1,0:T(8,128)(2,1)} %param.6) | copy-start | bytes 786436
  0.0 31.5 %slice-start = ((s8[6291456]{0:T(1024)(128)(4,1)}), s8[4194304]{0:T(1024)(128)(4,1)S(1)}, s32[]{:S(2)}) async-start(s8[6291456]{0:T(1024)(128)(4,1)} %bitcast.96), calls=%async_computation.22 | async-start | bytes 8388608
  21.5 32.5 %copy-start = (f32[2,1,4096]{2,1,0:T(1,128)S(1)}, f32[2,1,4096]{2,1,0:T(1,128)}, u32[]{:S(2)}) copy-start(f32[2,1,4096]{2,1,0:T(1,128)} %gain.21) | copy-start | bytes 98308
  21.5 10.0 %slice-start.1 = ((s8[6291456]{0:T(1024)(128)(4,1)}), s8[2097152]{0:T(1024)(128)(4,1)S(1)}, s32[]{:S(2)}) async-start(s8[6291456]{0:T(1024)(128)(4,1)} %bitcast.96), calls=%async_computation.23 | async-start | bytes 4194304
  21.5 1.9 collective-permute-start
  29.2 2.0 collective-permute-start.1
  31.3 37.1 %collective-permute-start.3 = (bf16[2,1,2,4096,384]{4,3,2,1,0:T(8,128)(2,1)}, bf16[2,1,2,4096,384]{4,3,2,1,0:T(8,128)(2,1)}, u32[]{:S(2)}, u32[]{:S(2)}) collective-permute-start(bf16[2,1,2,4096,384]{4,3,2,1,0:T(8,128)(2,1)} %w_in.3), channel_id=1, source_target_pairs={{0,1},{1,0},{2,3},{3,2},{4,5},{5,4},{6,7},{7,6},{8,9},{9,8},{10,11... | collective-permute-start | bytes 37748744 | tf_op jit(solution)/shard_map/ppermute | solution.py:259
  31.5 36.9 %collective-permute-start.4 = (bf16[2,1,384,4096]{3,2,1,0:T(8,128)(2,1)S(1)}, bf16[2,1,384,4096]{3,2,1,0:T(8,128)(2,1)}, u32[]{:S(2)}, u32[]{:S(2)}) collective-permute-start(bf16[2,1,384,4096]{3,2,1,0:T(8,128)(2,1)S(1)} %bitcast.97), channel_id=1, source_target_pairs={{0,1},{1,0},{2,3},{3,2},{4,5},{5,4},{6,7},{7,6},{8,9},{9,8},{10,11... | collective-permute-start | bytes 18874376 | tf_op jit(solution)/shard_map/ppermute | solution.py:259
  47.3 6.7 %collective-permute-start.2 = (bf16[32,4096]{1,0:T(8,128)(2,1)S(1)}, bf16[32,4096]{1,0:T(8,128)(2,1)S(1)}, u32[]{:S(2)}, u32[]{:S(2)}) collective-permute-start(bf16[32,4096]{1,0:T(8,128)(2,1)S(1)} %mix.11), channel_id=1, source_target_pairs={{0,32},{32,0},{64,96},{96,64},{1,33},{33,1},{65,97},{97,65},{2,34}... | collective-permute-start | bytes 786440 | tf_op jit(solution)/shard_map/ppermute | solution.py:321
  87.4 6.4 %collective-permute-start.5 = (bf16[32,4096]{1,0:T(8,128)(2,1)S(1)}, bf16[32,4096]{1,0:T(8,128)(2,1)S(1)}, u32[]{:S(2)}, u32[]{:S(2)}) collective-permute-start(bf16[32,4096]{1,0:T(8,128)(2,1)S(1)} %mix.12), channel_id=1, source_target_pairs={{0,32},{32,64},{64,96},{96,0},{1,33},{33,65},{65,97},{97,1},{2,34}... | collective-permute-start | bytes 786440 | tf_op jit(solution)/shard_map/ppermute | solution.py:321
  125.2 6.4 %collective-permute-start.6 = (bf16[32,4096]{1,0:T(8,128)(2,1)S(1)}, bf16[32,4096]{1,0:T(8,128)(2,1)S(1)}, u32[]{:S(2)}, u32[]{:S(2)}) collective-permute-start(bf16[32,4096]{1,0:T(8,128)(2,1)S(1)} %mix.13), channel_id=1, source_target_pairs={{0,32},{32,64},{64,96},{96,0},{1,33},{33,65},{65,97},{97,1},{2,34}... | collective-permute-start | bytes 786440 | tf_op jit(solution)/shard_map/ppermute | solution.py:321
  163.0 6.6 %collective-permute-start.7 = (bf16[32,4096]{1,0:T(8,128)(2,1)S(1)}, bf16[32,4096]{1,0:T(8,128)(2,1)S(1)}, u32[]{:S(2)}, u32[]{:S(2)}) collective-permute-start(bf16[32,4096]{1,0:T(8,128)(2,1)S(1)} %mix.14), channel_id=1, source_target_pairs={{0,32},{32,64},{64,96},{96,0},{1,33},{33,65},{65,97},{97,1},{2,34}... | collective-permute-start | bytes 786440 | tf_op jit(solution)/shard_map/ppermute | solution.py:321
  202.3 7.9 %collective-permute-start.8 = (bf16[32,4096]{1,0:T(8,128)(2,1)S(1)}, bf16[32,4096]{1,0:T(8,128)(2,1)S(1)}, u32[]{:S(2)}, u32[]{:S(2)}) collective-permute-start(bf16[32,4096]{1,0:T(8,128)(2,1)S(1)} %mix.15), channel_id=1, source_target_pairs={{0,32},{32,64},{64,96},{96,0},{1,33},{33,65},{65,97},{97,1},{2,34}... | collective-permute-start | bytes 786440 | tf_op jit(solution)/shard_map/ppermute | solution.py:321
  244.2 7.4 %collective-permute-start.9 = (bf16[32,4096]{1,0:T(8,128)(2,1)S(1)}, bf16[32,4096]{1,0:T(8,128)(2,1)S(1)}, u32[]{:S(2)}, u32[]{:S(2)}) collective-permute-start(bf16[32,4096]{1,0:T(8,128)(2,1)S(1)} %mix.16), channel_id=1, source_target_pairs={{0,32},{32,64},{64,96},{96,0},{1,33},{33,65},{65,97},{97,1},{2,34}... | collective-permute-start | bytes 786440 | tf_op jit(solution)/shard_map/ppermute | solution.py:321
  282.7 7.7 %collective-permute-start.10 = (bf16[32,4096]{1,0:T(8,128)(2,1)S(1)}, bf16[32,4096]{1,0:T(8,128)(2,1)S(1)}, u32[]{:S(2)}, u32[]{:S(2)}) collective-permute-start(bf16[32,4096]{1,0:T(8,128)(2,1)S(1)} %mix.17), channel_id=1, source_target_pairs={{0,32},{32,64},{64,96},{96,0},{1,33},{33,65},{65,97},{97,1},{2,34}... | collective-permute-start | bytes 786440 | tf_op jit(solution)/shard_map/ppermute | solution.py:321
  321.5 7.9 %collective-permute-start.11 = (bf16[32,4096]{1,0:T(8,128)(2,1)S(1)}, bf16[32,4096]{1,0:T(8,128)(2,1)S(1)}, u32[]{:S(2)}, u32[]{:S(2)}) collective-permute-start(bf16[32,4096]{1,0:T(8,128)(2,1)S(1)} %mix.18), channel_id=1, source_target_pairs={{0,32},{32,64},{64,96},{96,0},{1,33},{33,65},{65,97},{97,1},{2,34}... | collective-permute-start | bytes 786440 | tf_op jit(solution)/shard_map/ppermute | solution.py:321
  360.5 8.3 %collective-permute-start.12 = (bf16[32,4096]{1,0:T(8,128)(2,1)S(1)}, bf16[32,4096]{1,0:T(8,128)(2,1)S(1)}, u32[]{:S(2)}, u32[]{:S(2)}) collective-permute-start(bf16[32,4096]{1,0:T(8,128)(2,1)S(1)} %mix.19), channel_id=1, source_target_pairs={{0,0},{32,64},{64,96},{96,32},{1,1},{33,65},{65,97},{97,33},{2,2},... | collective-permute-start | bytes 786440 | tf_op jit(solution)/shard_map/ppermute | solution.py:321
  401.7 8.3 %collective-permute-start.13 = (bf16[32,4096]{1,0:T(8,128)(2,1)S(1)}, bf16[32,4096]{1,0:T(8,128)(2,1)S(1)}, u32[]{:S(2)}, u32[]{:S(2)}) collective-permute-start(bf16[32,4096]{1,0:T(8,128)(2,1)S(1)} %mix.20), channel_id=1, source_target_pairs={{0,0},{32,32},{64,96},{96,64},{1,1},{33,33},{65,97},{97,65},{2,2},... | collective-permute-start | bytes 786440 | tf_op jit(solution)/shard_map/ppermute | solution.py:321
